TPU v7x, 32 devices: a whole 2x2x4 slice. The times are simulated.
32 devices in a mesh: blk: 8 (over y, x, core), kv: 4 (over z).
Axes of the slice: x: 2, y: 2, z: 4, core: 2. Of those that a mesh axis runs over, the one named last changes fastest.
Arguments:
- tokens: bfloat16 [4096, 2560], P('blk'), may hold values from -6 to 6
- attn_gain: float32 [2560], replicated, may hold values from 0.1 to 1.9
- mlp_gain: float32 [2560], replicated, may hold values from 0.1 to 1.9
- w_query: float32 [2560, 2560], P(('blk', 'kv')), may hold values from -0.375 to 0.375
- w_key: float32 [2560, 640], P(('blk', 'kv')), may hold values from -0.125 to 0.125
- w_value: float32 [2560, 640], P(('blk', 'kv')), may hold values from -0.125 to 0.125
- w_gate: float32 [2560, 6912], P(('blk', 'kv')), may hold values from -0.125 to 0.125
- w_up: float32 [2560, 6912], P(('blk', 'kv')), may hold values from -0.125 to 0.125
- w_out: bfloat16 [2560, 2560], P('kv'), may hold values from -0.125 to 0.125
- w_down: bfloat16 [6912, 2560], P('kv'), may hold values from -0.078125 to 0.078125
- cache: bfloat16 [2, 64, 8, 80, 128], P(None, 'blk', 'kv'), may hold values from -300 to 300
- slot_prompt: int32 [64], replicated, may hold values from 0 to 7, as said below
- prefix_len: int32 [8], replicated, may hold values from 1 to 2048, as said below
- new_len: int32 [8], replicated, may hold values from 256 to 512, as said below
Outputs:
- mixed: bfloat16 [4096, 2560], P('blk', 'kv')
Inputs may be any that keep to these rules, and one draw needn't show every extreme that they name: `slot_prompt`: the 8 slots of one index of blk hold at most 2 blocks of one prompt. One prompt, drawn afresh, has exactly 2 blocks on every index of blk; the other 6 slots of an index hold blocks of distinct prompts; every prompt has at least one block. `prefix_len`: A prompt with c slots has a prefix longer than (c - 1) * 128 and at most c * 128. Rows i >= new_len[p] of prompt p are padding.
All inputs are finite; a program needn't handle non-finite values.
Results may differ from a plain program's by a relative error of at most 0.019.
The roundings to bfloat16 on the way count: a program that leaves them out, or rounds other values in their place, can miss the bound.
Values may be sent and summed in bfloat16 or wider, within the bound.
No kernel may reach another device: no remote copies, remote signals or barrier semaphores. Data moves between devices by JAX's collectives and lax.ppermute only.
A program may use at most 128 MiB of HBM per device.

v0:
```python
import functools
import math

import jax
import jax.numpy as jnp
from jax import lax
from jax.experimental import pallas as pl
from jax.experimental.pallas import tpu as pltpu
from jax.sharding import PartitionSpec as P

HEADS = 32
KV_HEADS = 8
HD = 80
WINDOW = 4096
SINKS = 4
BLOCK = 128
CAP = 2


FLOOR_SCORE = -1e30
EPSILON = 1e-05
ROPE_BASE = 10000.0
FAR = 1 << 30
LANES = 128
TILE = 256
ROW_TILE = 128
VMEM_LIMIT = 56 * 1024 * 1024

ANY = pl.BlockSpec(memory_space=pl.ANY)
VMEM = pl.BlockSpec(memory_space=pltpu.VMEM)
SMEM = pl.BlockSpec(memory_space=pltpu.SMEM)


def rms_scale(row_data, gain_vec):
    values = row_data.astype(jnp.float32)
    mean_square = jnp.mean(values * values, axis=-1, keepdims=True)
    return (values * lax.rsqrt(mean_square + EPSILON) * gain_vec).astype(jnp.bfloat16)


def rope_tables(positions):
    half_width = HD // 2
    frequency = ROPE_BASE ** (-2.0 * jnp.arange(half_width, dtype=jnp.float32) / HD)
    angles = positions.astype(jnp.float32)[:, None] * frequency[None, :]
    cosine = jnp.cos(angles)
    sine = jnp.sin(angles)
    return (
        jnp.concatenate([cosine, cosine], axis=1),
        jnp.concatenate([-sine, sine], axis=1),
    )


def slot_ranks(slot_prompt, prompts, slots):
    onehot = (slot_prompt[:, None] == jnp.arange(prompts, dtype=jnp.int32)[None, :]).astype(
        jnp.int32
    )
    running = jnp.cumsum(onehot, axis=0)
    global_rank = jnp.sum(onehot * (running - 1), axis=1)
    local_count = jnp.cumsum(onehot.reshape(-1, slots, prompts), axis=1).reshape(-1, prompts)
    local_rank = jnp.sum(onehot * (local_count - 1), axis=1)
    return (global_rank, local_rank)


def swap(values, axis, bit):
    pairs = [(index, index ^ bit) for index in range(lax.axis_size(axis))]
    return lax.ppermute(values, axis, pairs)


def half_up(width):
    return (width // 2 + LANES - 1) // LANES * LANES


def pack_kernel(layouts, groups, *refs):
    kv_index = lax.axis_index("kv")
    outs = refs[len(refs) - groups * len(layouts) :]
    for choice in range(groups):

        @pl.when(kv_index == choice)
        def _():
            for which, spans in enumerate(layouts):
                for other in range(groups):
                    out = outs[which * groups + other]
                    column = 0
                    for matrix, first, last in spans:
                        start = (choice ^ other) * (refs[matrix].shape[1] // groups)
                        width = last - first
                        out[:, column : column + width] = refs[matrix][
                            :, start + first : start + last
                        ].astype(jnp.bfloat16)
                        column += width


def pack(matrices, groups, layouts, name):
    rows = matrices[0].shape[0]
    shapes = []
    for spans in layouts:
        width = sum(last - first for _, first, last in spans)
        shapes += [jax.ShapeDtypeStruct((rows, width), jnp.bfloat16)] * groups
    flat = pl.pallas_call(
        functools.partial(pack_kernel, layouts, groups),
        out_shape=tuple(shapes),
        in_specs=[VMEM] * len(matrices),
        out_specs=(VMEM,) * len(shapes),
        compiler_params=pltpu.CompilerParams(vmem_limit_bytes=VMEM_LIMIT),
        cost_estimate=pl.CostEstimate(
            flops=0,
            bytes_accessed=6 * rows * sum(matrix.shape[1] for matrix in matrices),
            transcendentals=0,
        ),
        name=name,
    )(*matrices)
    return [flat[first : first + groups] for first in range(0, len(flat), groups)]


def exchange_in_order(parts, kv_index):
    moved = jnp.stack(
        [parts[0]] + [swap(part, "kv", other) for other, part in enumerate(parts) if other], axis=0
    )
    order = jnp.arange(len(parts), dtype=jnp.int32) ^ kv_index
    return jnp.take(moved, order, axis=0).reshape(-1, moved.shape[2])


def after(values, *earlier):
    return lax.optimization_barrier((values, *earlier))[0]


def on_columns(body, index, width, count):
    if width % LANES == 0:
        body(pl.ds(pl.multiple_of(index * width, LANES), width))
        return
    for choice in range(count):
        pl.when(index == choice)(functools.partial(body, pl.ds(choice * width, width)))


EXTRA = 16


def cache_kernel(blocks_ref, flags_ref, keys, values):
    first_row = lax.broadcasted_iota(jnp.int32, (EXTRA, 1), 0) == 0
    bias = jnp.where((flags_ref[...] > -FAR) | jnp.logical_not(first_row), 0.0, FLOOR_SCORE)
    for head in range(blocks_ref.shape[2]):
        keys[head, HD:, :] = bias.astype(jnp.bfloat16)
        for block in range(blocks_ref.shape[1]):
            place = pl.ds(block * BLOCK, BLOCK)
            keys[head, :HD, place] = blocks_ref[0, block, head]
            values[head, place, :] = blocks_ref[1, block, head].astype(jnp.float32).T.astype(
                jnp.bfloat16
            )


def cached_rows(blocks, flags):
    kv_local = blocks.shape[2]
    cached = flags.shape[1]
    return pl.pallas_call(
        cache_kernel,
        out_shape=(
            jax.ShapeDtypeStruct((kv_local, HD + EXTRA, cached), jnp.bfloat16),
            jax.ShapeDtypeStruct((kv_local, cached, HD), jnp.bfloat16),
        ),
        in_specs=[VMEM, VMEM],
        out_specs=(VMEM, VMEM),
        compiler_params=pltpu.CompilerParams(vmem_limit_bytes=VMEM_LIMIT),
        cost_estimate=pl.CostEstimate(
            flops=0, bytes_accessed=4 * blocks.size, transcendentals=0
        ),
        name="cached",
    )(blocks, flags)


def project_kernel(
    kv_local,
    per_group,
    normed_ref,
    cos_ref,
    sin_ref,
    flags_ref,
    source_ref,
    upper,
    lower,
    keys,
    values,
    weights,
    projected,
    sems,
):
    half = upper.shape[0]
    width = weights.shape[1]
    spans = [pl.ds(first, min(2 * TILE, width - first)) for first in range(0, width, 2 * TILE)]
    copies = [
        pltpu.make_async_copy(source_ref.at[:, columns], weights.at[:, columns], sems.at[at])
        for at, columns in enumerate(spans)
    ]
    for copy in copies:
        copy.start()
    new_rows = normed_ref.shape[0]
    chunk_rows = per_group * ROW_TILE
    first_row = lax.broadcasted_iota(jnp.int32, (EXTRA, 1), 0) == 0
    bias = jnp.where((flags_ref[...] > -FAR) | jnp.logical_not(first_row), 0.0, FLOOR_SCORE)
    marker = jnp.where(
        lax.broadcasted_iota(jnp.int32, (chunk_rows, EXTRA), 1) == 0, 1.0, 0.0
    ).astype(jnp.bfloat16)
    for head in range(kv_local):
        keys[head, HD:, :] = bias.astype(jnp.bfloat16)
        for chunk in range(half):
            upper[chunk, head, :, HD:] = marker
            lower[chunk, head, :, HD:] = marker
    for columns, copy in zip(spans, copies):
        copy.wait()
        projected[:, columns] = jnp.dot(
            normed_ref[...], weights[:, columns], preferred_element_type=jnp.float32
        )

    def rotated(rows, column):
        part = projected[rows, column : column + HD]
        turned = jnp.concatenate([part[:, HD // 2 :], part[:, : HD // 2]], axis=1)
        return part * cos_ref[rows, :] + turned * sin_ref[rows, :]

    query_width = kv_local * per_group * HD
    for chunk in range(new_rows // ROW_TILE):
        rows = pl.ds(chunk * ROW_TILE, ROW_TILE)
        for head in range(kv_local):
            for sub in range(per_group):
                queries = upper if chunk < half else lower
                queries[chunk % half, head, sub * ROW_TILE : (sub + 1) * ROW_TILE, :HD] = rotated(
                    rows, (head * per_group + sub) * HD
                ).astype(jnp.bfloat16)
            keys[head, :HD, rows] = rotated(rows, query_width + head * HD).T.astype(jnp.bfloat16)
            column = query_width + (kv_local + head) * HD
            values[head, rows, :] = projected[rows, column : column + HD].astype(jnp.bfloat16)


def project_rows(normed, tables, flags, weights, kv_local, per_group):
    new_rows = normed.shape[0]
    width = weights.shape[1]
    queries = jax.ShapeDtypeStruct(
        (new_rows // ROW_TILE // 2, kv_local, per_group * ROW_TILE, HD + EXTRA), jnp.bfloat16
    )
    upper, lower, keys, values = pl.pallas_call(
        functools.partial(project_kernel, kv_local, per_group),
        out_shape=(
            queries,
            queries,
            jax.ShapeDtypeStruct((kv_local, HD + EXTRA, new_rows), jnp.bfloat16),
            jax.ShapeDtypeStruct((kv_local, new_rows, HD), jnp.bfloat16),
        ),
        in_specs=[VMEM] * 4 + [ANY],
        out_specs=(VMEM,) * 4,
        scratch_shapes=[
            pltpu.VMEM((normed.shape[1], width), jnp.bfloat16),
            pltpu.VMEM((new_rows, width), jnp.float32),
            pltpu.SemaphoreType.DMA((width // TILE,)),
        ],
        compiler_params=pltpu.CompilerParams(vmem_limit_bytes=VMEM_LIMIT),
        cost_estimate=pl.CostEstimate(
            flops=2 * new_rows * normed.shape[1] * width,
            bytes_accessed=2 * normed.shape[1] * width,
            transcendentals=0,
        ),
        name="project",
    )(normed, *tables, flags, weights)
    return (upper, lower), (keys, values)


def attention_kernel(
    first_step,
    place_ref,
    queries,
    cached_keys,
    cached_values,
    own_keys,
    own_values,
    cached_ref,
    own_ref,
    out_ref,
    scores,
    probs,
    folded,
    shifts,
    summed,
):
    prefix_here = place_ref[1]
    kv_local, _, cached = cached_keys.shape
    new_rows = own_keys.shape[2]
    chunk_rows = queries.shape[2]
    per_group = chunk_rows // ROW_TILE
    factor = math.log2(math.e) / math.sqrt(HD)
    group = 64
    widest = min(4 * LANES, cached)
    tiles = [
        (first, cached_keys, cached_values, first, widest) for first in range(0, cached, widest)
    ]
    tiles.append((cached, own_keys, own_values, 0, new_rows))

    def score(step, head, first, keys, _, begin, width):
        scores[head, :, pl.ds(first, width)] = jnp.dot(
            queries[step, head],
            keys[head, :, pl.ds(begin, width)],
            preferred_element_type=jnp.float32,
        )
        own = keys is own_keys
        for part in range(chunk_rows // group):
            rows = pl.ds(part * group, group)
            if own:
                row_id = (first_step + step) * ROW_TILE + (part * group) % ROW_TILE + (
                    lax.broadcasted_iota(jnp.int32, (group, LANES), 0)
                )
            top = folded[head, rows, :]
            for lane in range(0, width, LANES):
                place = pl.ds(first + lane, LANES)
                piece = scores[head, rows, place]
                if own:
                    own_id = lane + lax.broadcasted_iota(jnp.int32, (group, LANES), 1)
                    piece = jnp.where(own_id <= row_id, piece, FLOOR_SCORE)
                    scores[head, rows, place] = piece
                top = jnp.maximum(top, piece)
            folded[head, rows, :] = top

    def narrow(step, head):
        def some(part, inner):
            rows = pl.ds(pl.multiple_of(part * 16, 16), 16)
            row_id = (first_step + step) * ROW_TILE + lax.rem(part * 16, ROW_TILE) + (
                lax.broadcasted_iota(jnp.int32, (16, 1), 0)
            )
            oldest = prefix_here + row_id - WINDOW
            old = jnp.where(cached_ref[...] > oldest, scores[head, rows, :cached], FLOOR_SCORE)
            new = jnp.where(own_ref[...] > oldest, scores[head, rows, cached:], FLOOR_SCORE)
            scores[head, rows, :cached] = old
            scores[head, rows, cached:] = new
            top = jnp.maximum(
                jnp.max(old, axis=1, keepdims=True), jnp.max(new, axis=1, keepdims=True)
            )
            folded[head, rows, :] = jnp.broadcast_to(top, (16, LANES))
            return inner

        lax.fori_loop(0, chunk_rows // 16, some, 0)

    def weigh(head, start, first, _, values, begin, width):
        for part in range(chunk_rows // group):
            rows = pl.ds(part * group, group)
            shift = shifts[head, rows, :]
            total = None if start else folded[head, rows, :]
            for lane in range(0, width, LANES):
                place = pl.ds(first + lane, LANES)
                piece = jnp.exp2(scores[head, rows, place] * factor - shift)
                total = piece if total is None else total + piece
                probs[head, rows, place] = piece.astype(jnp.bfloat16)
            folded[head, rows, :] = total
        return jnp.dot(
            probs[head, :, pl.ds(first, width)],
            values[head, pl.ds(begin, width), :],
            preferred_element_type=jnp.float32,
        )

    def attend(windowed, step, carry):
        for head in range(kv_local):
            folded[head] = jnp.full(folded.shape[1:], FLOOR_SCORE, jnp.float32)
            for tile in tiles:
                score(step, head, *tile)
        for head in range(kv_local):
            if windowed:
                narrow(step, head)
            for part in range(chunk_rows // group):
                rows = pl.ds(part * group, group)
                top = jnp.max(folded[head, rows, :], axis=1, keepdims=True) * factor
                shifts[head, rows, :] = jnp.broadcast_to(top, (group, LANES))
            for which, tile in enumerate(tiles):
                part = weigh(head, which == 0, *tile)
                summed[head] = part if which == 0 else summed[head] + part
            rows = pl.ds(pl.multiple_of(step * ROW_TILE, ROW_TILE), ROW_TILE)
            for sub in range(per_group):
                part = pl.ds(sub * ROW_TILE, ROW_TILE)
                total = jnp.sum(folded[head, part, :], axis=1, keepdims=True)
                column = (head * per_group + sub) * HD
                out_ref[rows, column : column + HD] = (summed[head, part, :] / total).astype(
                    jnp.bfloat16
                )
        return carry

    behind = prefix_here + new_rows > WINDOW
    for windowed in (False, True):

        @pl.when(behind == windowed)
        def _():
            lax.fori_loop(0, queries.shape[0], functools.partial(attend, windowed), 0)


def attend_rows(place, first_step, queries, cached, own, cached_pos, own_pos):
    chunks, kv_local, chunk_rows, _ = queries.shape
    span = cached_pos.shape[1] + own_pos.shape[1]
    heads = kv_local * chunk_rows // ROW_TILE
    new_rows = chunks * ROW_TILE
    return pl.pallas_call(
        functools.partial(attention_kernel, first_step),
        out_shape=jax.ShapeDtypeStruct((new_rows, heads * HD), jnp.bfloat16),
        in_specs=[SMEM] + [VMEM] * 7,
        out_specs=VMEM,
        scratch_shapes=[
            pltpu.VMEM((kv_local, chunk_rows, span), jnp.float32),
            pltpu.VMEM((kv_local, chunk_rows, span), jnp.bfloat16),
            pltpu.VMEM((kv_local, chunk_rows, LANES), jnp.float32),
            pltpu.VMEM((kv_local, chunk_rows, LANES), jnp.float32),
            pltpu.VMEM((kv_local, chunk_rows, HD), jnp.float32),
        ],
        compiler_params=pltpu.CompilerParams(vmem_limit_bytes=VMEM_LIMIT),
        cost_estimate=pl.CostEstimate(
            flops=8 * heads * new_rows * span * LANES,
            bytes_accessed=4 * span * LANES * kv_local,
            transcendentals=heads * new_rows * span,
        ),
        name="attention",
    )(place, queries, *cached, *own, cached_pos, own_pos)


def gather_groups(piece):
    groups = lax.axis_size("kv")
    pieces = {0: piece}
    for other in sorted(range(1, groups), key=lambda other: (bin(other).count("1"), -other)):
        low = other & -other
        near = pieces[low] if other ^ low else piece
        pieces[other] = swap(after(pieces[other ^ low], near), "kv", low)
    return [pieces[other] for other in range(groups)]


def sum_at_owner(parts):
    parts = list(parts)
    earlier = []
    for other in sorted(range(1, len(parts)), key=lambda other: -bin(other).count("1")):
        low = other & -other
        target = other ^ low
        came = swap(after(parts[other], *earlier), "kv", low)
        if target:
            earlier.append(came)
        added = parts[target].astype(jnp.float32) + came.astype(jnp.float32)
        parts[target] = added.astype(jnp.bfloat16) if target else added
    return parts[0]


def middle_kernel(sources, groups, place_ref, tokens_ref, gain_ref, *refs):
    parts = len(refs) - len(sources) - 7
    att = refs[:parts]
    own_ref = refs[parts]
    rest = refs[parts + 1 :]
    shares = rest[: len(sources)]
    normed_ref, residual_ref, gathered, weights, middle, sem = rest[len(sources) :]
    blk_index = place_ref[0]
    kv_index = place_ref[2]
    group_rows = own_ref.shape[0]
    new_rows, model = tokens_ref.shape
    tile = 2 * TILE
    loads = []
    for step in range(model // tile):
        columns = pl.ds(step * tile, tile)
        copies = []
        if shares[0].ndim == 3:
            copies.append((own_ref.at[:, columns], weights.at[pl.ds(0, group_rows), columns]))
            for (indices, _, _), ref in zip(sources, shares):
                part = ref.shape[1]
                for at, index in enumerate(indices):
                    first = pl.multiple_of((blk_index ^ index) * part, 16)
                    for other in range(1, groups):
                        lead = at * (groups - 1) + other - 1
                        rows = pl.ds(other * group_rows + first, part)
                        copies.append((ref.at[lead, :, columns], weights.at[rows, columns]))
        else:
            for other in range(groups):
                first = pl.multiple_of((kv_index ^ other) * group_rows, 16)
                rows = pl.ds(other * group_rows, group_rows)
                copies.append(
                    (shares[0].at[pl.ds(first, group_rows), columns], weights.at[rows, columns])
                )
        loads.append(
            [pltpu.make_async_copy(source, target, sem.at[step]) for source, target in copies]
        )
        for copy in loads[-1]:
            copy.start()
    some_rows, feature = att[0].shape
    for at, part in enumerate(att):
        first, other = at // groups * some_rows, at % groups
        gathered[first : first + some_rows, other * feature : (other + 1) * feature] = part[...]
    for step in range(model // tile):
        columns = pl.ds(step * tile, tile)
        for copy in loads[step]:
            copy.wait()
        summed = jnp.dot(gathered[...], weights[:, columns], preferred_element_type=jnp.float32)
        middle[:, columns] = (tokens_ref[:, columns].astype(jnp.float32) + summed).astype(
            jnp.bfloat16
        )

    def scale(step, carry):
        rows = pl.ds(pl.multiple_of(step * 16, 16), 16)
        part = middle[rows, :].astype(jnp.float32)
        mean_square = jnp.mean(part * part, axis=1, keepdims=True)
        normed_ref[rows, :] = (part * lax.rsqrt(mean_square + EPSILON) * gain_ref[...]).astype(
            jnp.bfloat16
        )
        return carry

    lax.fori_loop(0, new_rows // 16, scale, 0, unroll=2)
    out_width = model // groups

    def keep(columns):
        residual_ref[...] = middle[:, columns]

    on_columns(keep, kv_index, out_width, groups)


def middle_rows(place, tokens, gain, attended, own, sources, groups):
    new_rows, model = tokens.shape
    arrays = [values for _, _, values in sources]
    return pl.pallas_call(
        functools.partial(middle_kernel, sources, groups),
        out_shape=(
            jax.ShapeDtypeStruct((new_rows, model), jnp.bfloat16),
            jax.ShapeDtypeStruct((new_rows, model // groups), jnp.bfloat16),
        ),
        in_specs=[SMEM, VMEM, VMEM] + [VMEM] * len(attended) + [ANY] * (1 + len(arrays)),
        out_specs=(VMEM, VMEM),
        scratch_shapes=[
            pltpu.VMEM((new_rows, model), jnp.bfloat16),
            pltpu.VMEM((model, model), jnp.bfloat16),
            pltpu.VMEM((new_rows, model), jnp.bfloat16),
            pltpu.SemaphoreType.DMA((model // (2 * TILE),)),
        ],
        compiler_params=pltpu.CompilerParams(vmem_limit_bytes=VMEM_LIMIT),
        cost_estimate=pl.CostEstimate(
            flops=2 * new_rows * model * model,
            bytes_accessed=2 * model * model,
            transcendentals=0,
        ),
        name="middle",
    )(place, tokens, gain, *attended, own, *arrays)


def hidden_chunks(width):
    return [(first, min(TILE, width - first)) for first in range(0, width, TILE)]


def mlp_kernel(groups, widths, place_ref, normed_ref, down_ref, left, right, *refs):
    outs = refs[:groups]
    first_half, second_half, down, hidden, sems = refs[groups:]
    kv_index = place_ref[2]
    chunks = []
    base = 0
    for width, source, buffer in zip(widths, (left, right), (first_half, second_half)):
        for first, units in hidden_chunks(width):
            columns = pl.ds(2 * first, 2 * units)
            copy = pltpu.make_async_copy(
                source.at[:, columns], buffer.at[:, columns], sems.at[len(chunks)]
            )
            chunks.append((buffer, columns, base + first, units, copy))
        base += width
    last = pltpu.make_async_copy(down_ref, down, sems.at[len(chunks)])
    ahead = 3
    for _, _, _, _, copy in chunks[:ahead]:
        copy.start()
    for at, (buffer, columns, first, units, copy) in enumerate(chunks):
        copy.wait()
        if at + ahead < len(chunks):
            chunks[at + ahead][4].start()
        elif at + ahead == len(chunks):
            last.start()
        both = jnp.dot(normed_ref[...], buffer[:, columns], preferred_element_type=jnp.float32)
        gated, raised = both[:, :units], both[:, units:]
        hidden[:, first : first + units] = (gated / (1.0 + jnp.exp(-gated)) * raised).astype(
            jnp.bfloat16
        )
    last.wait()
    out_width = outs[0].shape[1]
    for other in range(groups):

        def product(columns, out=outs[other]):
            out[...] = jnp.dot(
                hidden[...], down[:, columns], preferred_element_type=jnp.float32
            ).astype(out.dtype)

        on_columns(product, kv_index ^ other, out_width, groups)


def mlp_parts(place, normed, w_down, left, right, groups, widths):
    new_rows, model = normed.shape
    out_width = model // groups
    return pl.pallas_call(
        functools.partial(mlp_kernel, groups, widths),
        out_shape=tuple(
            jax.ShapeDtypeStruct((new_rows, out_width), jnp.bfloat16 if other else jnp.float32)
            for other in range(groups)
        ),
        in_specs=[SMEM, VMEM, ANY, ANY, ANY],
        out_specs=(VMEM,) * groups,
        scratch_shapes=[
            pltpu.VMEM(left.shape, jnp.bfloat16),
            pltpu.VMEM(right.shape, jnp.bfloat16),
            pltpu.VMEM(w_down.shape, jnp.bfloat16),
            pltpu.VMEM((new_rows, w_down.shape[0]), jnp.bfloat16),
            pltpu.SemaphoreType.DMA((1 + sum(len(hidden_chunks(width)) for width in widths),)),
        ],
        compiler_params=pltpu.CompilerParams(vmem_limit_bytes=VMEM_LIMIT),
        cost_estimate=pl.CostEstimate(
            flops=6 * new_rows * model * w_down.shape[0],
            bytes_accessed=6 * model * w_down.shape[0],
            transcendentals=new_rows * w_down.shape[0],
        ),
        name="mlp",
    )(place, normed, w_down, left, right)


def shards(
    tokens,
    attn_gain,
    mlp_gain,
    w_query,
    w_key,
    w_value,
    w_gate,
    w_up,
    w_out,
    w_down,
    cache,
    slot_prompt,
    prefix_len,
    new_len,
):
    groups = lax.axis_size("kv")
    blk_index = lax.axis_index("blk")
    kv_index = lax.axis_index("kv")
    query_width = w_query.shape[1] // groups
    key_width = w_key.shape[1] // groups
    per_group = HEADS // KV_HEADS
    new_rows = tokens.shape[0]
    prompts = prefix_len.shape[0]
    slots = cache.shape[1]
    prefix_here = prefix_len[blk_index]
    live_count = new_len[blk_index]
    place = jnp.stack([blk_index, prefix_here, kv_index]).astype(jnp.int32)

    global_rank, local_rank = slot_ranks(slot_prompt, prompts, slots)
    own_prompts = lax.dynamic_slice_in_dim(slot_prompt, blk_index * slots, slots)
    own_ranks = lax.dynamic_slice_in_dim(local_rank, blk_index * slots, slots)
    placed = own_prompts * CAP + own_ranks
    buffer_ids = jnp.arange(prompts * CAP, dtype=jnp.int32)
    matches = placed[None, :] == buffer_ids[:, None]
    source_slot = jnp.sum(
        jnp.where(matches, jnp.arange(slots, dtype=jnp.int32)[None, :], 0), axis=1
    )
    outgoing = jnp.take(cache, source_slot, axis=1)
    arrived = lax.all_to_all(outgoing, "blk", split_axis=1, concat_axis=1, tiled=True)
    slot_ids = jnp.arange(prompts * slots, dtype=jnp.int32)
    landing = slot_ids // slots * CAP + local_rank
    for_me = slot_prompt == blk_index
    received = (landing[None, :] == buffer_ids[:, None]) & for_me[None, :]
    block_number = jnp.sum(jnp.where(received, global_rank[None, :], 0), axis=1)
    block_live = jnp.any(received, axis=1)
    key_pos = block_number[:, None] * BLOCK + jnp.arange(BLOCK, dtype=jnp.int32)[None, :]
    key_live = block_live[:, None] & (key_pos < prefix_here)
    cached_pos = jnp.where(key_live, jnp.where(key_pos < SINKS, FAR, key_pos), -FAR)
    cached_pos = cached_pos.reshape(1, -1)
    row_ids = jnp.arange(new_rows, dtype=jnp.int32)
    positions = prefix_here + row_ids
    own_pos = jnp.where(
        row_ids < live_count, jnp.where(positions < SINKS, FAR, positions), -FAR
    ).reshape(1, -1)

    normed = rms_scale(tokens, attn_gain)
    tables = rope_tables(positions)
    cached = cached_rows(arrived, cached_pos)

    hidden_width = w_gate.shape[1] // groups
    cut = hidden_width // (2 * TILE) * TILE
    widths = (cut, hidden_width - cut)
    layouts = []
    base = 0
    for width in widths:
        layout = []
        for first, units in hidden_chunks(width):
            start = base + first
            layout += [(0, start, start + units), (1, start, start + units)]
        layouts.append(layout)
        base += width
    packed = pack((w_gate, w_up), groups, layouts, "pack_pair")

    spans = [(0, 0, query_width), (1, 0, key_width), (2, 0, key_width)]
    (qkv_parts,) = pack((w_query, w_key, w_value), groups, [spans], "pack_qkv")
    moved_qkv = exchange_in_order(qkv_parts, kv_index)
    w_qkv = lax.all_gather(moved_qkv, "blk", axis=0, tiled=True)

    moved = exchange_in_order(after(packed[0], moved_qkv, arrived), kv_index)
    first_half = lax.all_gather(after(moved, w_qkv, *cached), "blk", axis=0, tiled=True)

    eighth = w_out.shape[0] // lax.axis_size("blk")
    spread = lax.axis_size("blk") == 8 and eighth % 16 == 0
    if spread:
        share = lax.dynamic_slice_in_dim(w_out, blk_index * eighth, eighth, 0)
        share = after(share, moved)
        shares = [swap(share, "kv", other) for other in range(1, groups)]

    queries, own = project_rows(normed, tables, own_pos, w_qkv, cache.shape[2], per_group)
    half = queries[0].shape[0]
    upper = attend_rows(place, 0, queries[0], cached, own, cached_pos, own_pos)
    moved_second = exchange_in_order(after(packed[1], upper), kv_index)
    if spread:
        shares = jnp.stack(after(shares, upper), axis=0)
        near = (swap(shares, "blk", 2), swap(shares, "blk", 4))
    lower = attend_rows(
        place, half, after(queries[1], upper), cached, own, cached_pos, own_pos
    )
    earlier = (lower, *near) if spread else (lower,)
    second_half = lax.all_gather(after(moved_second, *earlier), "blk", axis=0, tiled=True)
    attended = jnp.concatenate([upper, lower], axis=0)
    everyone = gather_groups(attended)

    if spread:
        by_x, by_y = near
        by_y = after(by_y, upper, lower)
        diagonal = swap(by_y, "blk", 2)
        trio = swap(jnp.concatenate([shares, by_x, by_y], axis=0), "blk", 1)
        w_out_sources = [
            ((0,), 0, shares),
            ((2,), 0, by_x),
            ((4,), 0, by_y),
            ((6,), 0, diagonal),
            ((1, 3, 5), 0, trio),
            ((7,), 0, swap(after(diagonal, everyone[-1]), "blk", 1)),
        ]
    else:
        w_out_sources = [(0, 0, lax.all_gather(w_out, "kv", axis=0, tiled=True))]

    normed_mid, residual = middle_rows(
        place, tokens, mlp_gain.reshape(1, -1), everyone, w_out, w_out_sources, groups
    )
    parts = mlp_parts(place, normed_mid, w_down, first_half, second_half, groups, widths)
    reduced = sum_at_owner(parts)
    mixed = jnp.where(
        (row_ids < live_count)[:, None], residual.astype(jnp.float32) + reduced, 0.0
    )
    return mixed.astype(jnp.bfloat16)


def solution(mesh):
    return jax.shard_map(
        shards,
        mesh=mesh,
        in_specs=(
            P("blk", None),
            P(),
            P(),
            P(("blk", "kv"), None),
            P(("blk", "kv"), None),
            P(("blk", "kv"), None),
            P(("blk", "kv"), None),
            P(("blk", "kv"), None),
            P("kv", None),
            P("kv", None),
            P(None, "blk", "kv", None, None),
            P(),
            P(),
            P(),
        ),
        out_specs=P("blk", "kv"),
        check_vma=False,
    )
```

profile of v0, /device:TPU:0, one launch (start us, length us, event | category | flops | bytes accessed | tf_op | source)
XLA Modules:
  0.0 326.7 jit_solution(14749463081332587913)
XLA Ops:
  6.5 2.3 pack_qkv.1
  8.8 5.0 %collective-permute-start.2 = (bf16[80,960]{1,0:T(8,128)(2,1)}, bf16[80,960]{1,0:T(8,128)(2,1)S(1)}, u32[]{:S(2)}, u32[]{:S(2)}) collective-permute-start(bf16[80,960]{1,0:T(8,128)(2,1)} %get-tuple-element.53), channel_id=1, source_target_pairs={{0,3},{1,2},{2,1},{3,0},{4,7},{5,6},{6,5},{7,4},{8,11},{9,10},{10,... | collective-permute-start | bytes 460808 | tf_op jit(solution)/shard_map/ppermute | solution.py:65
  14.6 4.6 %collective-permute-done.2 = bf16[80,960]{1,0:T(8,128)(2,1)S(1)} collective-permute-done((bf16[80,960]{1,0:T(8,128)(2,1)}, bf16[80,960]{1,0:T(8,128)(2,1)S(1)}, u32[]{:S(2)}, u32[]{:S(2)}) %collective-permute-start.2) | collective-permute-done | bytes 153632 | tf_op jit(solution)/shard_map/ppermute | solution.py:65
  19.2 8.8 %collective-permute-done.1 = bf16[80,960]{1,0:T(8,128)(2,1)S(1)} collective-permute-done((bf16[80,960]{1,0:T(8,128)(2,1)}, bf16[80,960]{1,0:T(8,128)(2,1)S(1)}, u32[]{:S(2)}, u32[]{:S(2)}) %collective-permute-start.1) | collective-permute-done | bytes 153632 | tf_op jit(solution)/shard_map/ppermute | solution.py:65
  32.2 1.3 select_bitcast_fusion
  33.5 3.9 %all-to-all-start = ((bf16[2,16,2,80,128]{4,3,2,0,1:T(8,128)(2,1)}), bf16[2,16,2,80,128]{4,3,2,0,1:T(8,128)(2,1)S(1)}, u32[]{:S(2)}, u32[]{:S(2)}) async-start(bf16[2,16,2,80,128]{4,3,2,0,1:T(8,128)(2,1)} %select_bitcast_fusion), calls=%async_computation | async-start | bytes 2621440 | tf_op jit(solution)/shard_map/all_to_all | solution.py:645
  38.2 4.7 %pack_pair.1 = (bf16[80,1536]{1,0:T(8,128)(2,1)}, bf16[80,1536]{1,0:T(8,128)(2,1)}, bf16[80,1536]{1,0:T(8,128)(2,1)}, bf16[80,1536]{1,0:T(8,128)(2,1)}, bf16[80,...) custom-call(f32[80,6912]{1,0:T(8,128)} %refs_0_.3, ...), custom_call_target="tpu_custom_call" | custom-call | bytes 6635520 | tf_op jit(solution)/shard_map/pack_pair/pallas_call | solution.py:98
  43.5 19.1 %all-to-all-done = bf16[2,16,2,80,128]{4,3,2,0,1:T(8,128)(2,1)S(1)} async-done(((bf16[2,16,2,80,128]{4,3,2,0,1:T(8,128)(2,1)}), bf16[2,16,2,80,128]{4,3,2,0,1:T(8,128)(2,1)S(1)}, u32[]{:S(2)}, u32[]{:S(2)}) %all-to-all-start) | async-done | bytes 1310752 | tf_op jit(solution)/shard_map/all_to_all | solution.py:645
  62.6 2.5 collective-permute-start.8
  65.0 1.9 collective-permute-start.6
  67.0 1.3 fusion.6.flags_ref.cached_ref
  68.2 1.2 copy.19.blocks_ref
  69.4 3.1 cached.1
  73.5 9.2 %collective-permute-done.7 = bf16[80,1536]{1,0:T(8,128)(2,1)S(1)} collective-permute-done((bf16[80,1536]{1,0:T(8,128)(2,1)}, bf16[80,1536]{1,0:T(8,128)(2,1)S(1)}, u32[]{:S(2)}, u32[]{:S(2)}) %collective-permute-start.7) | collective-permute-done | bytes 245792 | tf_op jit(solution)/shard_map/ppermute | solution.py:65
  83.5 1.2 bitcast_select_fusion.1
  85.9 1.3 pad_add_fusion.place_ref
  87.9 2.0 compare_select_fusion.2.flags_ref.own_ref
  93.5 2.2 fusion.2.normed_ref
  95.7 1.1 collective-permute-start.9
  96.8 2.4 collective-permute-start.10
  100.1 12.3 %project.1 = (bf16[2,2,512,96]{3,2,1,0:T(8,128)(2,1)}, bf16[2,2,512,96]{3,2,1,0:T(8,128)(2,1)}, bf16[2,96,512]{2,1,0:T(8,128)(2,1)}, bf16[2,512,80]{2,1,0:T(8,128)(2,1)}) custom-call(bf16[512,2560]{1,0:T(8,128)(2,1)} %fusion.2.normed_ref, f32[512,80]{1,0:T(8,128)} %get-tuple-element.98.cos_ref, f32[512,80]{1,0:T(8,128)} %get-tuple-element.99.sin_ref, ...), custom_call_target="tpu_custom_call" | custom-call | flops 2516582400 | bytes 4915200 | tf_op jit(solution)/shard_map/project/pallas_call | solution.py:237
  112.4 14.3 %attention.2 = bf16[256,640]{1,0:T(8,128)(2,1)} custom-call(s32[3]{0:T(128)} %pad_add_fusion.place_ref, bf16[2,2,512,96]{3,2,1,0:T(8,128)(2,1)} %get-tuple-element.54.queries, bf16[2,96,2048]{2,1,0:T(8,128)(2,1)} %get-tuple-element.55.cached_keys, bf16[2,2048,80]{2,1,0:T(8,128)(2,1)} %get-tuple-element.56.cached_values, ...), custom_call_target="tpu_custom_call" | custom-call | flops 5368709120 | bytes 2621440 | tf_op jit(solution)/shard_map/attention/pallas_call | solution.py:391
  127.6 1.3 pad_maximum_fusion.refs_5_
  128.9 2.4 collective-permute-start.12
  131.9 1.3 collective-permute-start.19
  133.3 14.0 %collective-permute-start.18 = (bf16[80,1920]{1,0:T(8,128)(2,1)S(1)}, bf16[80,1920]{1,0:T(8,128)(2,1)S(1)}, u32[]{:S(2)}, u32[]{:S(2)}) collective-permute-start(bf16[80,1920]{1,0:T(8,128)(2,1)S(1)} %copy-done.22), channel_id=1, source_target_pairs={{0,2},{1,3},{2,0},{3,1},{4,6},{5,7},{6,4},{7,5},{8,10},{9,11},{10,... | collective-permute-start | bytes 921608 | tf_op jit(solution)/shard_map/ppermute | solution.py:65
  147.4 13.9 %attention.3 = bf16[256,640]{1,0:T(8,128)(2,1)} custom-call(s32[3]{0:T(128)} %pad_add_fusion.place_ref, bf16[2,2,512,96]{3,2,1,0:T(8,128)(2,1)} %get-tuple-element.60.queries, bf16[2,96,2048]{2,1,0:T(8,128)(2,1)} %get-tuple-element.55.cached_keys, bf16[2,2048,80]{2,1,0:T(8,128)(2,1)} %get-tuple-element.56.cached_values, ...), custom_call_target="tpu_custom_call" | custom-call | flops 5368709120 | bytes 2621440 | tf_op jit(solution)/shard_map/attention/pallas_call | solution.py:391
  161.3 4.6 %collective-permute-done.18 = bf16[80,1920]{1,0:T(8,128)(2,1)S(1)} collective-permute-done((bf16[80,1920]{1,0:T(8,128)(2,1)S(1)}, bf16[80,1920]{1,0:T(8,128)(2,1)S(1)}, u32[]{:S(2)}, u32[]{:S(2)}) %collective-permute-start.18) | collective-permute-done | bytes 307232 | tf_op jit(solution)/shard_map/ppermute | solution.py:65
  166.9 1.3 bitcast_select_fusion
  169.3 1.4 constant_dynamic-update-slice_fusion.1
  170.7 1.4 constant_dynamic-update-slice_fusion
  172.3 3.8 %collective-permute-start.3 = (bf16[512,640]{1,0:T(8,128)(2,1)S(1)}, bf16[512,640]{1,0:T(8,128)(2,1)S(1)}, u32[]{:S(2)}, u32[]{:S(2)}) collective-permute-start(bf16[512,640]{1,0:T(8,128)(2,1)S(1)} %pad_maximum_fusion.4.refs_0_), channel_id=1, source_target_pairs={{0,1},{1,0},{2,3},{3,2},{4,5},{5,4},{6,7},{7,6},{8,9},{9,8},{10,11... | collective-permute-start | bytes 1966088 | tf_op jit(solution)/shard_map/ppermute | solution.py:65
  176.1 1.6 collective-permute-start.4
  178.2 27.3 %collective-permute-done.3.refs_1_ = bf16[512,640]{1,0:T(8,128)(2,1)S(1)} collective-permute-done((bf16[512,640]{1,0:T(8,128)(2,1)S(1)}, bf16[512,640]{1,0:T(8,128)(2,1)S(1)}, u32[]{:S(2)}, u32[]{:S(2)}) %collective-permute-start.3) | collective-permute-done | bytes 655392 | tf_op jit(solution)/shard_map/ppermute | solution.py:65
  205.5 3.3 collective-permute-start.5
  208.8 14.6 %collective-permute-done.5.refs_3_ = bf16[512,640]{1,0:T(8,128)(2,1)S(1)} collective-permute-done((bf16[512,640]{1,0:T(8,128)(2,1)S(1)}, bf16[512,640]{1,0:T(8,128)(2,1)S(1)}, u32[]{:S(2)}, u32[]{:S(2)}) %collective-permute-start.5) | collective-permute-done | bytes 655392 | tf_op jit(solution)/shard_map/ppermute | solution.py:65
  223.3 1.8 collective-permute-done.14.refs_8_
  226.2 1.8 collective-permute-done.16.refs_10_
  229.1 1.8 copy-done.15
  230.9 15.9 %middle.1 = (bf16[512,2560]{1,0:T(8,128)(2,1)}, bf16[512,640]{1,0:T(8,128)(2,1)}) custom-call(s32[3]{0:T(128)} %pad_add_fusion.place_ref, bf16[512,2560]{1,0:T(8,128)(2,1)} %tokens_ref.1, f32[1,2560]{1,0:T(1,128)} %reshape.191.gain_ref, bf16[512,640]{1,0:T(8,128)(2,1)} %copy-done.6, bf16[512,640]{1,0:T(8,128)(2,1)} %copy-done.18, ...), custom_call_target="tpu_custom_call" | custom-call | flops 6710886400 | bytes 13107200 | tf_op jit(solution)/shard_map/middle/pallas_call | solution.py:509
  246.9 1.3 all-gather.8.cloned.1.call-done.right
  248.2 21.1 %mlp.1 = (f32[512,640]{1,0:T(8,128)}, bf16[512,640]{1,0:T(8,128)(2,1)}, bf16[512,640]{1,0:T(8,128)(2,1)}, bf16[512,640]{1,0:T(8,128)(2,1)}) custom-call(s32[3]{0:T(128)} %pad_add_fusion.place_ref, bf16[512,2560]{1,0:T(8,128)(2,1)} %get-tuple-element.78.normed_ref, bf16[1728,2560]{1,0:T(8,128)(2,1)} %down_ref.1, ...), custom_call_target="tpu_custom_call" | custom-call | flops 13589544960 | bytes 26542080 | tf_op jit(solution)/shard_map/mlp/pallas_call | solution.py:581
  269.3 1.7 collective-permute-start.20
  271.1 15.4 %collective-permute-done.20 = bf16[512,640]{1,0:T(8,128)(2,1)S(1)} collective-permute-done((bf16[512,640]{1,0:T(8,128)(2,1)}, bf16[512,640]{1,0:T(8,128)(2,1)S(1)}, u32[]{:S(2)}, u32[]{:S(2)}) %collective-permute-start.20) | collective-permute-done | bytes 655392 | tf_op jit(solution)/shard_map/ppermute | solution.py:65
  286.5 1.2 add_convert_fusion
  287.7 1.1 collective-permute-start.22
  290.4 28.4 %collective-permute-done.22 = bf16[512,640]{1,0:T(8,128)(2,1)S(1)} collective-permute-done((bf16[512,640]{1,0:T(8,128)(2,1)S(1)}, bf16[512,640]{1,0:T(8,128)(2,1)S(1)}, u32[]{:S(2)}, u32[]{:S(2)}) %collective-permute-start.22) | collective-permute-done | bytes 655392 | tf_op jit(solution)/shard_map/ppermute | solution.py:65
  318.8 1.2 select_convert_fusion
  (130 shorter events, 22.4 us)
Async XLA Ops:
  6.5 24.9 %copy-start = (bf16[2,8,2,80,128]{4,3,2,1,0:T(8,128)(2,1)S(1)}, bf16[2,8,2,80,128]{4,3,2,1,0:T(8,128)(2,1)}, u32[]{:S(2)}) copy-start(bf16[2,8,2,80,128]{4,3,2,1,0:T(8,128)(2,1)} %param.24) | copy-start | bytes 1966084
  6.5 78.1 %all-gather.4.cloned.1.call-start = ((), (), s32[]{:S(2)}) async-start(), calls=%async_computation.1 | async-start | bytes 5898240 | tf_op jit(solution)/shard_map/all_gather | solution.py:683
  8.8 10.4 %collective-permute-start.2 = (bf16[80,960]{1,0:T(8,128)(2,1)}, bf16[80,960]{1,0:T(8,128)(2,1)S(1)}, u32[]{:S(2)}, u32[]{:S(2)}) collective-permute-start(bf16[80,960]{1,0:T(8,128)(2,1)} %get-tuple-element.53), channel_id=1, source_target_pairs={{0,3},{1,2},{2,1},{3,0},{4,7},{5,6},{6,5},{7,4},{8,11},{9,10},{10,... | collective-permute-start | bytes 460808 | tf_op jit(solution)/shard_map/ppermute | solution.py:65
  13.9 14.1 %collective-permute-start.1 = (bf16[80,960]{1,0:T(8,128)(2,1)}, bf16[80,960]{1,0:T(8,128)(2,1)S(1)}, u32[]{:S(2)}, u32[]{:S(2)}) collective-permute-start(bf16[80,960]{1,0:T(8,128)(2,1)} %get-tuple-element.52), channel_id=1, source_target_pairs={{0,2},{1,3},{2,0},{3,1},{4,6},{5,7},{6,4},{7,5},{8,10},{9,11},{10,... | collective-permute-start | bytes 460808 | tf_op jit(solution)/shard_map/ppermute | solution.py:65
  13.9 14.1 %collective-permute-start = (bf16[80,960]{1,0:T(8,128)(2,1)}, bf16[80,960]{1,0:T(8,128)(2,1)S(1)}, u32[]{:S(2)}, u32[]{:S(2)}) collective-permute-start(bf16[80,960]{1,0:T(8,128)(2,1)} %get-tuple-element.51), channel_id=1, source_target_pairs={{0,1},{1,0},{2,3},{3,2},{4,5},{5,4},{6,7},{7,6},{8,9},{9,8},{10,11... | collective-permute-start | bytes 460808 | tf_op jit(solution)/shard_map/ppermute | solution.py:65
  33.5 4.1 %copy-start.24 = (s32[8]{0:T(128)S(1)}, s32[8]{0:T(128)}, u32[]{:S(2)}) copy-start(s32[8]{0:T(128)} %param.26) | copy-start | bytes 100
  33.5 29.0 %all-to-all-start = ((bf16[2,16,2,80,128]{4,3,2,0,1:T(8,128)(2,1)}), bf16[2,16,2,80,128]{4,3,2,0,1:T(8,128)(2,1)S(1)}, u32[]{:S(2)}, u32[]{:S(2)}) async-start(bf16[2,16,2,80,128]{4,3,2,0,1:T(8,128)(2,1)} %select_bitcast_fusion), calls=%async_computation | async-start | bytes 2621440 | tf_op jit(solution)/shard_map/all_to_all | solution.py:645
  37.4 209.5 %all-gather.6.cloned.1.call-start = ((), (), s32[]{:S(2)}) async-start(), calls=%async_computation.2 | async-start | bytes 8847360 | tf_op jit(solution)/shard_map/all_gather | solution.py:686
  62.6 10.9 %collective-permute-start.8 = (bf16[80,1536]{1,0:T(8,128)(2,1)}, bf16[80,1536]{1,0:T(8,128)(2,1)S(1)}, u32[]{:S(2)}, u32[]{:S(2)}) collective-permute-start(bf16[80,1536]{1,0:T(8,128)(2,1)} %get-tuple-element.70), channel_id=1, source_target_pairs={{0,3},{1,2},{2,1},{3,0},{4,7},{5,6},{6,5},{7,4},{8,11},{9,10},{10,... | collective-permute-start | bytes 737288 | tf_op jit(solution)/shard_map/ppermute | solution.py:65
  65.0 17.7 %collective-permute-start.7 = (bf16[80,1536]{1,0:T(8,128)(2,1)}, bf16[80,1536]{1,0:T(8,128)(2,1)S(1)}, u32[]{:S(2)}, u32[]{:S(2)}) collective-permute-start(bf16[80,1536]{1,0:T(8,128)(2,1)} %get-tuple-element.69), channel_id=1, source_target_pairs={{0,2},{1,3},{2,0},{3,1},{4,6},{5,7},{6,4},{7,5},{8,10},{9,11},{10,... | collective-permute-start | bytes 737288 | tf_op jit(solution)/shard_map/ppermute | solution.py:65
  65.0 17.7 %collective-permute-start.6 = (bf16[80,1536]{1,0:T(8,128)(2,1)}, bf16[80,1536]{1,0:T(8,128)(2,1)S(1)}, u32[]{:S(2)}, u32[]{:S(2)}) collective-permute-start(bf16[80,1536]{1,0:T(8,128)(2,1)} %get-tuple-element.68), channel_id=1, source_target_pairs={{0,1},{1,0},{2,3},{3,2},{4,5},{5,4},{6,7},{7,6},{8,9},{9,8},{10,11... | collective-permute-start | bytes 737288 | tf_op jit(solution)/shard_map/ppermute | solution.py:65
  69.4 13.3 %copy-start.11 = (bf16[80,1536]{1,0:T(8,128)(2,1)S(1)}, bf16[80,1536]{1,0:T(8,128)(2,1)}, u32[]{:S(2)}) copy-start(bf16[80,1536]{1,0:T(8,128)(2,1)} %get-tuple-element.67) | copy-start | bytes 737284
  83.5 1.7 copy-start.25
  84.6 7.2 %copy-start.2 = (bf16[512,2560]{1,0:T(8,128)(2,1)S(1)}, bf16[512,2560]{1,0:T(8,128)(2,1)}, u32[]{:S(2)}) copy-start(bf16[512,2560]{1,0:T(8,128)(2,1)} %tokens_ref.1) | copy-start | bytes 7864324
  84.7 163.5 %all-gather.8.cloned.1.call-start = ((), (), s32[]{:S(2)}) async-start(), calls=%async_computation.3 | async-start | bytes 11059200 | tf_op jit(solution)/shard_map/all_gather | solution.py:706
  91.8 1.7 copy-start.13
  95.7 31.1 %collective-permute-start.9 = (bf16[80,2560]{1,0:T(8,128)(2,1)S(1)}, bf16[80,2560]{1,0:T(8,128)(2,1)S(1)}, u32[]{:S(2)}, u32[]{:S(2)}) collective-permute-start(bf16[80,2560]{1,0:T(8,128)(2,1)S(1)} %constant_dynamic-slice_fusion), channel_id=1, source_target_pairs={{0,1},{1,0},{2,3},{3,2},{4,5},{5,4},{6,7},{7,6},{8,9},{9,8},{10,11... | collective-permute-start | bytes 1228808 | tf_op jit(solution)/shard_map/ppermute | solution.py:65
  96.8 30.8 %collective-permute-start.10 = (bf16[80,2560]{1,0:T(8,128)(2,1)S(1)}, bf16[80,2560]{1,0:T(8,128)(2,1)S(1)}, u32[]{:S(2)}, u32[]{:S(2)}) collective-permute-start(bf16[80,2560]{1,0:T(8,128)(2,1)S(1)} %constant_dynamic-slice_fusion), channel_id=1, source_target_pairs={{0,2},{1,3},{2,0},{3,1},{4,6},{5,7},{6,4},{7,5},{8,10},{9,11},{10,... | collective-permute-start | bytes 1228808 | tf_op jit(solution)/shard_map/ppermute | solution.py:65
  99.2 28.4 %collective-permute-start.11 = (bf16[80,2560]{1,0:T(8,128)(2,1)S(1)}, bf16[80,2560]{1,0:T(8,128)(2,1)S(1)}, u32[]{:S(2)}, u32[]{:S(2)}) collective-permute-start(bf16[80,2560]{1,0:T(8,128)(2,1)S(1)} %constant_dynamic-slice_fusion), channel_id=1, source_target_pairs={{0,3},{1,2},{2,1},{3,0},{4,7},{5,6},{6,5},{7,4},{8,11},{9,10},{10,... | collective-permute-start | bytes 1228808 | tf_op jit(solution)/shard_map/ppermute | solution.py:65
  126.7 5.2 %copy-start.23 = (bf16[80,1920]{1,0:T(8,128)(2,1)S(1)}, bf16[80,1920]{1,0:T(8,128)(2,1)}, u32[]{:S(2)}) copy-start(bf16[80,1920]{1,0:T(8,128)(2,1)} %get-tuple-element.87) | copy-start | bytes 921604
  126.7 6.5 %copy-start.22 = (bf16[80,1920]{1,0:T(8,128)(2,1)S(1)}, bf16[80,1920]{1,0:T(8,128)(2,1)}, u32[]{:S(2)}) copy-start(bf16[80,1920]{1,0:T(8,128)(2,1)} %get-tuple-element.86) | copy-start | bytes 921604
  126.7 20.6 %copy-start.21 = (bf16[80,1920]{1,0:T(8,128)(2,1)S(1)}, bf16[80,1920]{1,0:T(8,128)(2,1)}, u32[]{:S(2)}) copy-start(bf16[80,1920]{1,0:T(8,128)(2,1)} %get-tuple-element.85) | copy-start | bytes 921604
  127.6 33.7 %copy-start.3 = (bf16[80,2560]{1,0:T(8,128)(2,1)}, bf16[80,2560]{1,0:T(8,128)(2,1)S(1)}, u32[]{:S(2)}) copy-start(bf16[80,2560]{1,0:T(8,128)(2,1)S(1)} %collective-permute-done.11) | copy-start | bytes 1228804
  128.9 39.3 %collective-permute-start.12 = (bf16[3,80,2560]{2,1,0:T(8,128)(2,1)}, bf16[3,80,2560]{2,1,0:T(8,128)(2,1)}, u32[]{:S(2)}, u32[]{:S(2)}) collective-permute-start(bf16[3,80,2560]{2,1,0:T(8,128)(2,1)} %pad_maximum_fusion.refs_5_), channel_id=1, source_target_pairs={{0,8},{4,12},{8,0},{12,4},{16,24},{20,28},{24,16},{28,20},{1,9},{5... | collective-permute-start | bytes 3686408 | tf_op jit(solution)/shard_map/ppermute | solution.py:65
  131.3 37.0 %collective-permute-start.13 = (bf16[3,80,2560]{2,1,0:T(8,128)(2,1)}, bf16[3,80,2560]{2,1,0:T(8,128)(2,1)}, u32[]{:S(2)}, u32[]{:S(2)}) collective-permute-start(bf16[3,80,2560]{2,1,0:T(8,128)(2,1)} %pad_maximum_fusion.refs_5_), channel_id=1, source_target_pairs={{0,16},{4,20},{8,24},{12,28},{16,0},{20,4},{24,8},{28,12},{1,17},{... | collective-permute-start | bytes 3686408 | tf_op jit(solution)/shard_map/ppermute | solution.py:65
  131.9 34.0 %copy-start.10 = (bf16[80,1920]{1,0:T(8,128)(2,1)S(1)}, bf16[80,1920]{1,0:T(8,128)(2,1)}, u32[]{:S(2)}) copy-start(bf16[80,1920]{1,0:T(8,128)(2,1)} %get-tuple-element.84) | copy-start | bytes 921604
  131.9 29.4 %collective-permute-start.19 = (bf16[80,1920]{1,0:T(8,128)(2,1)S(1)}, bf16[80,1920]{1,0:T(8,128)(2,1)S(1)}, u32[]{:S(2)}, u32[]{:S(2)}) collective-permute-start(bf16[80,1920]{1,0:T(8,128)(2,1)S(1)} %copy-done.23), channel_id=1, source_target_pairs={{0,3},{1,2},{2,1},{3,0},{4,7},{5,6},{6,5},{7,4},{8,11},{9,10},{10,... | collective-permute-start | bytes 921608 | tf_op jit(solution)/shard_map/ppermute | solution.py:65
  133.3 32.7 %collective-permute-start.18 = (bf16[80,1920]{1,0:T(8,128)(2,1)S(1)}, bf16[80,1920]{1,0:T(8,128)(2,1)S(1)}, u32[]{:S(2)}, u32[]{:S(2)}) collective-permute-start(bf16[80,1920]{1,0:T(8,128)(2,1)S(1)} %copy-done.22), channel_id=1, source_target_pairs={{0,2},{1,3},{2,0},{3,1},{4,6},{5,7},{6,4},{7,5},{8,10},{9,11},{10,... | collective-permute-start | bytes 921608 | tf_op jit(solution)/shard_map/ppermute | solution.py:65
  147.3 18.6 %collective-permute-start.17 = (bf16[80,1920]{1,0:T(8,128)(2,1)S(1)}, bf16[80,1920]{1,0:T(8,128)(2,1)S(1)}, u32[]{:S(2)}, u32[]{:S(2)}) collective-permute-start(bf16[80,1920]{1,0:T(8,128)(2,1)S(1)} %copy-done.21), channel_id=1, source_target_pairs={{0,1},{1,0},{2,3},{3,2},{4,5},{5,4},{6,7},{7,6},{8,9},{9,8},{10,11... | collective-permute-start | bytes 921608 | tf_op jit(solution)/shard_map/ppermute | solution.py:65
  170.6 1.5 copy-start.8
  170.6 1.5 copy-start.9
  170.7 54.5 %copy-start.12 = (f32[2560]{0:T(1024)S(1)}, f32[2560]{0:T(1024)}, u32[]{:S(2)}) copy-start(f32[2560]{0:T(1024)} %param.16) | copy-start | bytes 30724
  172.1 57.0 %collective-permute-start.15 = (bf16[9,80,2560]{2,1,0:T(8,128)(2,1)S(1)}, bf16[9,80,2560]{2,1,0:T(8,128)(2,1)S(1)}, u32[]{:S(2)}, u32[]{:S(2)}) collective-permute-start(bf16[9,80,2560]{2,1,0:T(8,128)(2,1)S(1)} %constant_dynamic-update-slice_fusion), channel_id=1, source_target_pairs={{0,4},{4,0},{8,12},{12,8},{16,20},{20,16},{24,28},{28,24},{1,5},{5... | collective-permute-start | bytes 11059208 | tf_op jit(solution)/shard_map/ppermute | solution.py:65
  172.3 56.8 %copy-start.6 = (bf16[512,640]{1,0:T(8,128)(2,1)}, bf16[512,640]{1,0:T(8,128)(2,1)S(1)}, u32[]{:S(2)}) copy-start(bf16[512,640]{1,0:T(8,128)(2,1)S(1)} %pad_maximum_fusion.4.refs_0_) | copy-start | bytes 1966084
  172.3 33.2 %collective-permute-start.3 = (bf16[512,640]{1,0:T(8,128)(2,1)S(1)}, bf16[512,640]{1,0:T(8,128)(2,1)S(1)}, u32[]{:S(2)}, u32[]{:S(2)}) collective-permute-start(bf16[512,640]{1,0:T(8,128)(2,1)S(1)} %pad_maximum_fusion.4.refs_0_), channel_id=1, source_target_pairs={{0,1},{1,0},{2,3},{3,2},{4,5},{5,4},{6,7},{7,6},{8,9},{9,8},{10,11... | collective-permute-start | bytes 1966088 | tf_op jit(solution)/shard_map/ppermute | solution.py:65
  176.1 29.4 %collective-permute-start.4 = (bf16[512,640]{1,0:T(8,128)(2,1)S(1)}, bf16[512,640]{1,0:T(8,128)(2,1)S(1)}, u32[]{:S(2)}, u32[]{:S(2)}) collective-permute-start(bf16[512,640]{1,0:T(8,128)(2,1)S(1)} %pad_maximum_fusion.4.refs_0_), channel_id=1, source_target_pairs={{0,2},{1,3},{2,0},{3,1},{4,6},{5,7},{6,4},{7,5},{8,10},{9,11},{10,... | collective-permute-start | bytes 1966088 | tf_op jit(solution)/shard_map/ppermute | solution.py:65
  177.7 47.4 %collective-permute-start.14 = (bf16[3,80,2560]{2,1,0:T(8,128)(2,1)}, bf16[3,80,2560]{2,1,0:T(8,128)(2,1)S(1)}, u32[]{:S(2)}, u32[]{:S(2)}) collective-permute-start(bf16[3,80,2560]{2,1,0:T(8,128)(2,1)} %collective-permute-done.13.refs_7_), channel_id=1, source_target_pairs={{0,8},{4,12},{8,0},{12,4},{16,24},{20,28},{24,16},{28,20},{1,9},{5... | collective-permute-start | bytes 3686408 | tf_op jit(solution)/shard_map/ppermute | solution.py:65
  205.5 17.9 %copy-start.18 = (bf16[512,640]{1,0:T(8,128)(2,1)}, bf16[512,640]{1,0:T(8,128)(2,1)S(1)}, u32[]{:S(2)}) copy-start(bf16[512,640]{1,0:T(8,128)(2,1)S(1)} %collective-permute-done.3.refs_1_) | copy-start | bytes 1966084
  205.5 17.8 %copy-start.19 = (bf16[512,640]{1,0:T(8,128)(2,1)}, bf16[512,640]{1,0:T(8,128)(2,1)S(1)}, u32[]{:S(2)}) copy-start(bf16[512,640]{1,0:T(8,128)(2,1)S(1)} %collective-permute-done.4.refs_2_) | copy-start | bytes 1966084
  205.5 17.8 %collective-permute-start.5 = (bf16[512,640]{1,0:T(8,128)(2,1)S(1)}, bf16[512,640]{1,0:T(8,128)(2,1)S(1)}, u32[]{:S(2)}, u32[]{:S(2)}) collective-permute-start(bf16[512,640]{1,0:T(8,128)(2,1)S(1)} %collective-permute-done.4.refs_2_), channel_id=1, source_target_pairs={{0,1},{1,0},{2,3},{3,2},{4,5},{5,4},{6,7},{7,6},{8,9},{9,8},{10,11... | collective-permute-start | bytes 1966088 | tf_op jit(solution)/shard_map/ppermute | solution.py:65
  223.3 4.7 %copy-start.20 = (bf16[512,640]{1,0:T(8,128)(2,1)}, bf16[512,640]{1,0:T(8,128)(2,1)S(1)}, u32[]{:S(2)}) copy-start(bf16[512,640]{1,0:T(8,128)(2,1)S(1)} %collective-permute-done.5.refs_3_) | copy-start | bytes 1966084
  225.1 2.9 collective-permute-start.16
  229.1 1.8 copy-start.15
  269.3 49.5 %copy-start.5 = (f32[512,640]{1,0:T(8,128)S(1)}, f32[512,640]{1,0:T(8,128)}, u32[]{:S(2)}) copy-start(f32[512,640]{1,0:T(8,128)} %get-tuple-element.89) | copy-start | bytes 3932164
  269.3 49.5 %copy-start.7 = (bf16[512,640]{1,0:T(8,128)(2,1)S(1)}, bf16[512,640]{1,0:T(8,128)(2,1)}, u32[]{:S(2)}) copy-start(bf16[512,640]{1,0:T(8,128)(2,1)} %get-tuple-element.77) | copy-start | bytes 1966084
  269.3 17.2 %collective-permute-start.20 = (bf16[512,640]{1,0:T(8,128)(2,1)}, bf16[512,640]{1,0:T(8,128)(2,1)S(1)}, u32[]{:S(2)}, u32[]{:S(2)}) collective-permute-start(bf16[512,640]{1,0:T(8,128)(2,1)} %get-tuple-element.91), channel_id=1, source_target_pairs={{0,1},{1,0},{2,3},{3,2},{4,5},{5,4},{6,7},{7,6},{8,9},{9,8},{10,11... | collective-permute-start | bytes 1966088 | tf_op jit(solution)/shard_map/ppermute | solution.py:65
  287.7 31.1 %collective-permute-start.22 = (bf16[512,640]{1,0:T(8,128)(2,1)S(1)}, bf16[512,640]{1,0:T(8,128)(2,1)S(1)}, u32[]{:S(2)}, u32[]{:S(2)}) collective-permute-start(bf16[512,640]{1,0:T(8,128)(2,1)S(1)} %add_convert_fusion), channel_id=1, source_target_pairs={{0,2},{1,3},{2,0},{3,1},{4,6},{5,7},{6,4},{7,5},{8,10},{9,11},{10,... | collective-permute-start | bytes 1966088 | tf_op jit(solution)/shard_map/ppermute | solution.py:65
  288.8 30.0 %collective-permute-start.21 = (bf16[512,640]{1,0:T(8,128)(2,1)}, bf16[512,640]{1,0:T(8,128)(2,1)S(1)}, u32[]{:S(2)}, u32[]{:S(2)}) collective-permute-start(bf16[512,640]{1,0:T(8,128)(2,1)} %get-tuple-element.92), channel_id=1, source_target_pairs={{0,1},{1,0},{2,3},{3,2},{4,5},{5,4},{6,7},{7,6},{8,9},{9,8},{10,11... | collective-permute-start | bytes 1966088 | tf_op jit(solution)/shard_map/ppermute | solution.py:65
  (5 other events, 5.4 us)
Sparse Core Ops, SparseCore 0:
  30.7 53.5 all-gather.3
  86.2 56.9 all-gather.5
  168.4 79.7 all-gather.7
where the time goes:
time: 332 us; the launch traced here: 327 us
  waiting for transfers between devices  139 us (42%)
  Pallas kernels  87.7 us (26%)
  starting transfers between devices  50.3 us (15%)
  other arithmetic  21.8 us (7%)
  local copies, waits for them, and re-layouts  14.6 us (4%)
  between operations  13.7 us (4%)
    ppermute x23, waiting for transfers between devices, swap(): return lax.ppermute(values, axis, pairs)  118 us
    ppermute x23, starting transfers between devices, swap(): return lax.ppermute(values, axis, pairs)  45.9 us
    pallas_call x2, Pallas kernels, attend_rows(): pl.pallas_call(functools.partial(attention_kernel, first_step), out_shape...  28.2 us
    pallas_call x1, Pallas kernels, mlp_parts(): pl.pallas_call(functools.partial(mlp_kernel, groups, widths), out_shape=t...  21.1 us
    all_to_all x1, waiting for transfers between devices, shards(): lax.all_to_all(outgoing, 'blk', split_axis=1, concat_axis=1, tiled=True)  19.1 us
    pallas_call x1, Pallas kernels, middle_rows(): pl.pallas_call(functools.partial(middle_kernel, sources, groups), out_sha...  15.9 us
    pallas_call x1, Pallas kernels, project_rows(): pl.pallas_call(functools.partial(project_kernel, kv_local, per_group), ou...  12.3 us
    pallas_call x2, Pallas kernels, pack(): pl.pallas_call(functools.partial(pack_kernel, layouts, groups), out_shape...  6.96 us
  transfers between devices with their start and end apart: 27, of which 14 were waited for; matrix products, arithmetic and copies ran while one was open for 8% of the time, Pallas kernels for 20%

commit v1 on v0

--- a/solution.py
+++ b/solution.py
@@ -415,8 +415,8 @@
     pieces = {0: piece}
     for other in sorted(range(1, groups), key=lambda other: (bin(other).count("1"), -other)):
         low = other & -other
-        near = pieces[low] if other ^ low else piece
-        pieces[other] = swap(after(pieces[other ^ low], near), "kv", low)
+        source = piece if other == low else after(pieces[other ^ low], pieces[low])
+        pieces[other] = swap(source, "kv", low)
     return [pieces[other] for other in range(groups)]
 
 
@@ -534,31 +534,28 @@
     return [(first, min(TILE, width - first)) for first in range(0, width, TILE)]
 
 
-def mlp_kernel(groups, widths, place_ref, normed_ref, down_ref, left, right, *refs):
+def mlp_kernel(groups, place_ref, normed_ref, down_ref, pair_ref, *refs):
     outs = refs[:groups]
-    first_half, second_half, down, hidden, sems = refs[groups:]
+    pair, down, hidden, sems = refs[groups:]
     kv_index = place_ref[2]
     chunks = []
-    base = 0
-    for width, source, buffer in zip(widths, (left, right), (first_half, second_half)):
-        for first, units in hidden_chunks(width):
-            columns = pl.ds(2 * first, 2 * units)
-            copy = pltpu.make_async_copy(
-                source.at[:, columns], buffer.at[:, columns], sems.at[len(chunks)]
-            )
-            chunks.append((buffer, columns, base + first, units, copy))
-        base += width
+    for first, units in hidden_chunks(down_ref.shape[0]):
+        columns = pl.ds(2 * first, 2 * units)
+        copy = pltpu.make_async_copy(
+            pair_ref.at[:, columns], pair.at[:, columns], sems.at[len(chunks)]
+        )
+        chunks.append((columns, first, units, copy))
     last = pltpu.make_async_copy(down_ref, down, sems.at[len(chunks)])
     ahead = 3
-    for _, _, _, _, copy in chunks[:ahead]:
+    for _, _, _, copy in chunks[:ahead]:
         copy.start()
-    for at, (buffer, columns, first, units, copy) in enumerate(chunks):
+    for at, (columns, first, units, copy) in enumerate(chunks):
         copy.wait()
         if at + ahead < len(chunks):
-            chunks[at + ahead][4].start()
+            chunks[at + ahead][3].start()
         elif at + ahead == len(chunks):
             last.start()
-        both = jnp.dot(normed_ref[...], buffer[:, columns], preferred_element_type=jnp.float32)
+        both = jnp.dot(normed_ref[...], pair[:, columns], preferred_element_type=jnp.float32)
         gated, raised = both[:, :units], both[:, units:]
         hidden[:, first : first + units] = (gated / (1.0 + jnp.exp(-gated)) * raised).astype(
             jnp.bfloat16
@@ -575,23 +572,22 @@
         on_columns(product, kv_index ^ other, out_width, groups)
 
 
-def mlp_parts(place, normed, w_down, left, right, groups, widths):
+def mlp_parts(place, normed, w_down, pair, groups):
     new_rows, model = normed.shape
     out_width = model // groups
     return pl.pallas_call(
-        functools.partial(mlp_kernel, groups, widths),
+        functools.partial(mlp_kernel, groups),
         out_shape=tuple(
             jax.ShapeDtypeStruct((new_rows, out_width), jnp.bfloat16 if other else jnp.float32)
             for other in range(groups)
         ),
-        in_specs=[SMEM, VMEM, ANY, ANY, ANY],
+        in_specs=[SMEM, VMEM, ANY, ANY],
         out_specs=(VMEM,) * groups,
         scratch_shapes=[
-            pltpu.VMEM(left.shape, jnp.bfloat16),
-            pltpu.VMEM(right.shape, jnp.bfloat16),
+            pltpu.VMEM(pair.shape, jnp.bfloat16),
             pltpu.VMEM(w_down.shape, jnp.bfloat16),
             pltpu.VMEM((new_rows, w_down.shape[0]), jnp.bfloat16),
-            pltpu.SemaphoreType.DMA((1 + sum(len(hidden_chunks(width)) for width in widths),)),
+            pltpu.SemaphoreType.DMA((1 + len(hidden_chunks(w_down.shape[0])),)),
         ],
         compiler_params=pltpu.CompilerParams(vmem_limit_bytes=VMEM_LIMIT),
         cost_estimate=pl.CostEstimate(
@@ -600,7 +596,7 @@
             transcendentals=new_rows * w_down.shape[0],
         ),
         name="mlp",
-    )(place, normed, w_down, left, right)
+    )(place, normed, w_down, pair)
 
 
 def shards(
@@ -664,26 +660,19 @@
     cached = cached_rows(arrived, cached_pos)
 
     hidden_width = w_gate.shape[1] // groups
-    cut = hidden_width // (2 * TILE) * TILE
-    widths = (cut, hidden_width - cut)
-    layouts = []
-    base = 0
-    for width in widths:
-        layout = []
-        for first, units in hidden_chunks(width):
-            start = base + first
-            layout += [(0, start, start + units), (1, start, start + units)]
-        layouts.append(layout)
-        base += width
-    packed = pack((w_gate, w_up), groups, layouts, "pack_pair")
+    layout = []
+    for first, units in hidden_chunks(hidden_width):
+        layout += [(0, first, first + units), (1, first, first + units)]
+    (packed,) = pack((w_gate, w_up), groups, [layout], "pack_pair")
 
     spans = [(0, 0, query_width), (1, 0, key_width), (2, 0, key_width)]
     (qkv_parts,) = pack((w_query, w_key, w_value), groups, [spans], "pack_qkv")
     moved_qkv = exchange_in_order(qkv_parts, kv_index)
     w_qkv = lax.all_gather(moved_qkv, "blk", axis=0, tiled=True)
 
-    moved = exchange_in_order(after(packed[0], moved_qkv, arrived), kv_index)
-    first_half = lax.all_gather(after(moved, w_qkv, *cached), "blk", axis=0, tiled=True)
+    moved = exchange_in_order(after(packed, moved_qkv, arrived), kv_index)
+    meanwhile = (*cached, normed, *tables, own_pos, place)
+    pair = lax.all_gather(after(moved, w_qkv, *meanwhile), "blk", axis=0, tiled=True)
 
     eighth = w_out.shape[0] // lax.axis_size("blk")
     spread = lax.axis_size("blk") == 8 and eighth % 16 == 0
@@ -695,21 +684,18 @@
     queries, own = project_rows(normed, tables, own_pos, w_qkv, cache.shape[2], per_group)
     half = queries[0].shape[0]
     upper = attend_rows(place, 0, queries[0], cached, own, cached_pos, own_pos)
-    moved_second = exchange_in_order(after(packed[1], upper), kv_index)
     if spread:
         shares = jnp.stack(after(shares, upper), axis=0)
         near = (swap(shares, "blk", 2), swap(shares, "blk", 4))
     lower = attend_rows(
         place, half, after(queries[1], upper), cached, own, cached_pos, own_pos
     )
-    earlier = (lower, *near) if spread else (lower,)
-    second_half = lax.all_gather(after(moved_second, *earlier), "blk", axis=0, tiled=True)
     attended = jnp.concatenate([upper, lower], axis=0)
     everyone = gather_groups(attended)
 
     if spread:
         by_x, by_y = near
-        by_y = after(by_y, upper, lower)
+        by_x, by_y = after((by_x, by_y), everyone[1], everyone[2])
         diagonal = swap(by_y, "blk", 2)
         trio = swap(jnp.concatenate([shares, by_x, by_y], axis=0), "blk", 1)
         w_out_sources = [
@@ -726,7 +712,7 @@
     normed_mid, residual = middle_rows(
         place, tokens, mlp_gain.reshape(1, -1), everyone, w_out, w_out_sources, groups
     )
-    parts = mlp_parts(place, normed_mid, w_down, first_half, second_half, groups, widths)
+    parts = mlp_parts(place, normed_mid, w_down, pair, groups)
     reduced = sum_at_owner(parts)
     mixed = jnp.where(
         (row_ids < live_count)[:, None], residual.astype(jnp.float32) + reduced, 0.0

time: 332 us -> 364 us (1.096)
  waiting for transfers between devices: 139 us -> 175 us
    ppermute x23 -> x20, waiting for transfers between devices: 118 us -> 164 us  [swap(): return lax.ppermute(values, axis, pairs)]
    all_to_all x1, waiting for transfers between devices: 19.1 us -> 10.5 us  [shards(): lax.all_to_all(outgoing, 'blk', split_axis=1, concat_axis=1, tiled=True)]
    ppermute x23 -> x20, starting transfers between devices: 45.9 us -> 44.6 us  [swap(): return lax.ppermute(values, axis, pairs)]
  transfers between devices with their start and end apart: 27 -> 23, of which waited for: 14 -> 13; matrix products, arithmetic and copies ran while one was open for 8% -> 7% of each run, Pallas kernels for 20% -> 18%
where the time goes in v1:
time: 364 us; the launch traced here: 360 us
  waiting for transfers between devices  175 us (48%)
  Pallas kernels  87.8 us (24%)
  starting transfers between devices  48.4 us (13%)
  other arithmetic  22.4 us (6%)
  between operations  14.2 us (4%)
  local copies, waits for them, and re-layouts  12.6 us (3%)
    ppermute x20, waiting for transfers between devices, swap(): return lax.ppermute(values, axis, pairs)  164 us
    ppermute x20, starting transfers between devices, swap(): return lax.ppermute(values, axis, pairs)  44.6 us
    pallas_call x2, Pallas kernels, attend_rows(): pl.pallas_call(functools.partial(attention_kernel, first_step), out_shape...  27.3 us
    pallas_call x1, Pallas kernels, mlp_parts(): pl.pallas_call(functools.partial(mlp_kernel, groups), out_shape=tuple((ja...  21.1 us
    pallas_call x1, Pallas kernels, middle_rows(): pl.pallas_call(functools.partial(middle_kernel, sources, groups), out_sha...  15.8 us
    pallas_call x1, Pallas kernels, project_rows(): pl.pallas_call(functools.partial(project_kernel, kv_local, per_group), ou...  12.8 us
    all_to_all x1, waiting for transfers between devices, shards(): lax.all_to_all(outgoing, 'blk', split_axis=1, concat_axis=1, tiled=True)  10.5 us
    pallas_call x2, Pallas kernels, pack(): pl.pallas_call(functools.partial(pack_kernel, layouts, groups), out_shape...  7.64 us
  transfers between devices with their start and end apart: 23, of which 13 were waited for; matrix products, arithmetic and copies ran while one was open for 7% of the time, Pallas kernels for 18%

profile of v1, /device:TPU:0, one launch (start us, length us, event | category | flops | bytes accessed | tf_op | source)
XLA Modules:
  0.0 359.9 jit_solution(10357033450318018431)
XLA Ops:
  6.5 2.3 pack_qkv.1
  8.9 3.0 collective-permute-start
  11.9 2.6 collective-permute-start.1
  14.7 4.1 %collective-permute-done = bf16[80,960]{1,0:T(8,128)(2,1)S(1)} collective-permute-done((bf16[80,960]{1,0:T(8,128)(2,1)}, bf16[80,960]{1,0:T(8,128)(2,1)S(1)}, u32[]{:S(2)}, u32[]{:S(2)}) %collective-permute-start) | collective-permute-done | bytes 153632 | tf_op jit(solution)/shard_map/ppermute | solution.py:65
  18.8 8.4 %collective-permute-done.1 = bf16[80,960]{1,0:T(8,128)(2,1)S(1)} collective-permute-done((bf16[80,960]{1,0:T(8,128)(2,1)}, bf16[80,960]{1,0:T(8,128)(2,1)S(1)}, u32[]{:S(2)}, u32[]{:S(2)}) %collective-permute-start.1) | collective-permute-done | bytes 153632 | tf_op jit(solution)/shard_map/ppermute | solution.py:65
  31.4 1.2 select_bitcast_fusion
  32.6 3.7 %all-to-all-start = ((bf16[2,16,2,80,128]{4,3,2,0,1:T(8,128)(2,1)}), bf16[2,16,2,80,128]{4,3,2,0,1:T(8,128)(2,1)S(1)}, u32[]{:S(2)}, u32[]{:S(2)}) async-start(bf16[2,16,2,80,128]{4,3,2,0,1:T(8,128)(2,1)} %select_bitcast_fusion), calls=%async_computation | async-start | bytes 2621440 | tf_op jit(solution)/shard_map/all_to_all | solution.py:641
  37.9 5.3 %pack_pair.1 = (bf16[80,3456]{1,0:T(8,128)(2,1)}, bf16[80,3456]{1,0:T(8,128)(2,1)}, bf16[80,3456]{1,0:T(8,128)(2,1)}, bf16[80,3456]{1,0:T(8,128)(2,1)}) custom-call(f32[80,6912]{1,0:T(8,128)} %refs_0_.3, f32[80,6912]{1,0:T(8,128)} %refs_1_.3), custom_call_target="tpu_custom_call" | custom-call | bytes 6635520 | tf_op jit(solution)/shard_map/pack_pair/pallas_call | solution.py:98
  45.3 1.0 pad_maximum_fusion.4
  47.0 1.9 compare_select_fusion.2.flags_ref.own_ref
  49.0 2.1 fusion.2.normed_ref
  51.1 10.5 %all-to-all-done = bf16[2,16,2,80,128]{4,3,2,0,1:T(8,128)(2,1)S(1)} async-done(((bf16[2,16,2,80,128]{4,3,2,0,1:T(8,128)(2,1)}), bf16[2,16,2,80,128]{4,3,2,0,1:T(8,128)(2,1)S(1)}, u32[]{:S(2)}, u32[]{:S(2)}) %all-to-all-start) | async-done | bytes 1310752 | tf_op jit(solution)/shard_map/all_to_all | solution.py:641
  61.6 2.6 collective-permute-start.6
  65.2 1.5 collective-permute-start.8
  66.8 1.3 pad_add_fusion.place_ref
  68.0 1.2 fusion.6.flags_ref.cached_ref
  69.3 1.1 copy.19.blocks_ref
  70.4 3.1 cached.1
  73.5 10.4 %collective-permute-done.6 = bf16[80,3456]{1,0:T(8,128)(2,1)S(1)} collective-permute-done((bf16[80,3456]{1,0:T(8,128)(2,1)}, bf16[80,3456]{1,0:T(8,128)(2,1)S(1)}, u32[]{:S(2)}, u32[]{:S(2)}) %collective-permute-start.6) | collective-permute-done | bytes 552992 | tf_op jit(solution)/shard_map/ppermute | solution.py:65
  83.9 20.4 %collective-permute-done.7 = bf16[80,3456]{1,0:T(8,128)(2,1)S(1)} collective-permute-done((bf16[80,3456]{1,0:T(8,128)(2,1)S(1)}, bf16[80,3456]{1,0:T(8,128)(2,1)S(1)}, u32[]{:S(2)}, u32[]{:S(2)}) %collective-permute-start.7) | collective-permute-done | bytes 552992 | tf_op jit(solution)/shard_map/ppermute | solution.py:65
  104.6 2.2 gather_fusion.2
  106.8 3.3 bitcast_select_fusion
  110.1 1.0 constant_dynamic-slice_fusion
  111.1 9.2 %collective-permute-start.10 = (bf16[80,2560]{1,0:T(8,128)(2,1)S(1)}, bf16[80,2560]{1,0:T(8,128)(2,1)S(1)}, u32[]{:S(2)}, u32[]{:S(2)}) collective-permute-start(bf16[80,2560]{1,0:T(8,128)(2,1)S(1)} %constant_dynamic-slice_fusion), channel_id=1, source_target_pairs={{0,2},{1,3},{2,0},{3,1},{4,6},{5,7},{6,4},{7,5},{8,10},{9,11},{10,... | collective-permute-start | bytes 1228808 | tf_op jit(solution)/shard_map/ppermute | solution.py:65
  120.4 1.4 collective-permute-start.11
  121.7 12.8 %project.1 = (bf16[2,2,512,96]{3,2,1,0:T(8,128)(2,1)}, bf16[2,2,512,96]{3,2,1,0:T(8,128)(2,1)}, bf16[2,96,512]{2,1,0:T(8,128)(2,1)}, bf16[2,512,80]{2,1,0:T(8,128)(2,1)}) custom-call(bf16[512,2560]{1,0:T(8,128)(2,1)} %fusion.2.normed_ref, f32[512,80]{1,0:T(8,128)} %get-tuple-element.80.cos_ref, f32[512,80]{1,0:T(8,128)} %get-tuple-element.81.sin_ref, ...), custom_call_target="tpu_custom_call" | custom-call | flops 2516582400 | bytes 4915200 | tf_op jit(solution)/shard_map/project/pallas_call | solution.py:237
  134.5 13.5 %attention.2 = bf16[256,640]{1,0:T(8,128)(2,1)} custom-call(s32[3]{0:T(128)} %pad_add_fusion.place_ref, bf16[2,2,512,96]{3,2,1,0:T(8,128)(2,1)} %get-tuple-element.45.queries, bf16[2,96,2048]{2,1,0:T(8,128)(2,1)} %get-tuple-element.46.cached_keys, bf16[2,2048,80]{2,1,0:T(8,128)(2,1)} %get-tuple-element.47.cached_values, ...), custom_call_target="tpu_custom_call" | custom-call | flops 5368709120 | bytes 2621440 | tf_op jit(solution)/shard_map/attention/pallas_call | solution.py:391
  148.2 4.0 %collective-permute-start.12 = (bf16[3,80,2560]{2,1,0:T(8,128)(2,1)S(1)}, bf16[3,80,2560]{2,1,0:T(8,128)(2,1)S(1)}, u32[]{:S(2)}, u32[]{:S(2)}) collective-permute-start(bf16[3,80,2560]{2,1,0:T(8,128)(2,1)S(1)} %pad_maximum_fusion.1.refs_5_), channel_id=1, source_target_pairs={{0,8},{4,12},{8,0},{12,4},{16,24},{20,28},{24,16},{28,20},{1,9},{5... | collective-permute-start | bytes 3686408 | tf_op jit(solution)/shard_map/ppermute | solution.py:65
  152.3 13.8 %attention.3 = bf16[256,640]{1,0:T(8,128)(2,1)} custom-call(s32[3]{0:T(128)} %pad_add_fusion.place_ref, bf16[2,2,512,96]{3,2,1,0:T(8,128)(2,1)} %get-tuple-element.51.queries, bf16[2,96,2048]{2,1,0:T(8,128)(2,1)} %get-tuple-element.46.cached_keys, bf16[2,2048,80]{2,1,0:T(8,128)(2,1)} %get-tuple-element.47.cached_values, ...), custom_call_target="tpu_custom_call" | custom-call | flops 5368709120 | bytes 2621440 | tf_op jit(solution)/shard_map/attention/pallas_call | solution.py:391
  166.1 1.1 pad_maximum_fusion.3.refs_0_
  167.2 7.4 %collective-permute-start.3 = (bf16[512,640]{1,0:T(8,128)(2,1)S(1)}, bf16[512,640]{1,0:T(8,128)(2,1)S(1)}, u32[]{:S(2)}, u32[]{:S(2)}) collective-permute-start(bf16[512,640]{1,0:T(8,128)(2,1)S(1)} %pad_maximum_fusion.3.refs_0_), channel_id=1, source_target_pairs={{0,1},{1,0},{2,3},{3,2},{4,5},{5,4},{6,7},{7,6},{8,9},{9,8},{10,11... | collective-permute-start | bytes 1966088 | tf_op jit(solution)/shard_map/ppermute | solution.py:65
  174.7 25.7 %collective-permute-done.3.refs_1_ = bf16[512,640]{1,0:T(8,128)(2,1)S(1)} collective-permute-done((bf16[512,640]{1,0:T(8,128)(2,1)S(1)}, bf16[512,640]{1,0:T(8,128)(2,1)S(1)}, u32[]{:S(2)}, u32[]{:S(2)}) %collective-permute-start.3) | collective-permute-done | bytes 655392 | tf_op jit(solution)/shard_map/ppermute | solution.py:65
  200.4 4.1 %collective-permute-done.4.refs_2_ = bf16[512,640]{1,0:T(8,128)(2,1)S(1)} collective-permute-done((bf16[512,640]{1,0:T(8,128)(2,1)S(1)}, bf16[512,640]{1,0:T(8,128)(2,1)S(1)}, u32[]{:S(2)}, u32[]{:S(2)}) %collective-permute-start.4) | collective-permute-done | bytes 655392 | tf_op jit(solution)/shard_map/ppermute | solution.py:65
  206.6 3.6 %collective-permute-start.5 = (bf16[512,640]{1,0:T(8,128)(2,1)S(1)}, bf16[512,640]{1,0:T(8,128)(2,1)S(1)}, u32[]{:S(2)}, u32[]{:S(2)}) collective-permute-start(bf16[512,640]{1,0:T(8,128)(2,1)S(1)} %collective-permute-done.4.refs_2_), channel_id=1, source_target_pairs={{0,1},{1,0},{2,3},{3,2},{4,5},{5,4},{6,7},{7,6},{8,9},{9,8},{10,11... | collective-permute-start | bytes 1966088 | tf_op jit(solution)/shard_map/ppermute | solution.py:65
  210.3 14.7 %collective-permute-done.5.refs_3_ = bf16[512,640]{1,0:T(8,128)(2,1)S(1)} collective-permute-done((bf16[512,640]{1,0:T(8,128)(2,1)S(1)}, bf16[512,640]{1,0:T(8,128)(2,1)S(1)}, u32[]{:S(2)}, u32[]{:S(2)}) %collective-permute-start.5) | collective-permute-done | bytes 655392 | tf_op jit(solution)/shard_map/ppermute | solution.py:65
  225.0 28.8 %collective-permute-done.14.refs_8_ = bf16[3,80,2560]{2,1,0:T(8,128)(2,1)S(1)} collective-permute-done((bf16[3,80,2560]{2,1,0:T(8,128)(2,1)S(1)}, bf16[3,80,2560]{2,1,0:T(8,128)(2,1)S(1)}, u32[]{:S(2)}, u32[]{:S(2)}) %collective-permute-start.14) | collective-permute-done | bytes 1228832 | tf_op jit(solution)/shard_map/ppermute | solution.py:65
  254.4 2.3 collective-permute-done.16.refs_10_
  256.7 1.0 copy-done.16
  257.7 1.9 copy-done.14
  259.7 15.8 %middle.1 = (bf16[512,2560]{1,0:T(8,128)(2,1)}, bf16[512,640]{1,0:T(8,128)(2,1)}) custom-call(s32[3]{0:T(128)} %pad_add_fusion.place_ref, bf16[512,2560]{1,0:T(8,128)(2,1)} %tokens_ref.1, f32[1,2560]{1,0:T(1,128)} %reshape.188.gain_ref, bf16[512,640]{1,0:T(8,128)(2,1)} %copy-done.7, bf16[512,640]{1,0:T(8,128)(2,1)} %copy-done.17, ...), custom_call_target="tpu_custom_call" | custom-call | flops 6710886400 | bytes 13107200 | tf_op jit(solution)/shard_map/middle/pallas_call | solution.py:509
  275.5 21.1 %mlp.1 = (f32[512,640]{1,0:T(8,128)}, bf16[512,640]{1,0:T(8,128)(2,1)}, bf16[512,640]{1,0:T(8,128)(2,1)}, bf16[512,640]{1,0:T(8,128)(2,1)}) custom-call(s32[3]{0:T(128)} %pad_add_fusion.place_ref, bf16[512,2560]{1,0:T(8,128)(2,1)} %get-tuple-element.69.normed_ref, bf16[1728,2560]{1,0:T(8,128)(2,1)} %down_ref.1, ...), custom_call_target="tpu_custom_call" | custom-call | flops 13589544960 | bytes 26542080 | tf_op jit(solution)/shard_map/mlp/pallas_call | solution.py:578
  296.7 5.8 %collective-permute-start.17 = (bf16[512,640]{1,0:T(8,128)(2,1)}, bf16[512,640]{1,0:T(8,128)(2,1)S(1)}, u32[]{:S(2)}, u32[]{:S(2)}) collective-permute-start(bf16[512,640]{1,0:T(8,128)(2,1)} %get-tuple-element.73), channel_id=1, source_target_pairs={{0,1},{1,0},{2,3},{3,2},{4,5},{5,4},{6,7},{7,6},{8,9},{9,8},{10,11... | collective-permute-start | bytes 1966088 | tf_op jit(solution)/shard_map/ppermute | solution.py:65
  302.5 15.2 %collective-permute-done.17 = bf16[512,640]{1,0:T(8,128)(2,1)S(1)} collective-permute-done((bf16[512,640]{1,0:T(8,128)(2,1)}, bf16[512,640]{1,0:T(8,128)(2,1)S(1)}, u32[]{:S(2)}, u32[]{:S(2)}) %collective-permute-start.17) | collective-permute-done | bytes 655392 | tf_op jit(solution)/shard_map/ppermute | solution.py:65
  317.7 1.7 collective-permute-start.18
  319.4 1.3 add_convert_fusion
  321.5 23.8 %collective-permute-done.18 = bf16[512,640]{1,0:T(8,128)(2,1)S(1)} collective-permute-done((bf16[512,640]{1,0:T(8,128)(2,1)}, bf16[512,640]{1,0:T(8,128)(2,1)S(1)}, u32[]{:S(2)}, u32[]{:S(2)}) %collective-permute-start.18) | collective-permute-done | bytes 655392 | tf_op jit(solution)/shard_map/ppermute | solution.py:65
  345.3 6.1 %collective-permute-done.19 = bf16[512,640]{1,0:T(8,128)(2,1)S(1)} collective-permute-done((bf16[512,640]{1,0:T(8,128)(2,1)S(1)}, bf16[512,640]{1,0:T(8,128)(2,1)S(1)}, u32[]{:S(2)}, u32[]{:S(2)}) %collective-permute-start.19) | collective-permute-done | bytes 655392 | tf_op jit(solution)/shard_map/ppermute | solution.py:65
  351.5 1.2 select_convert_fusion
  (114 shorter events, 13.8 us)
Async XLA Ops:
  6.5 24.0 %copy-start = (bf16[2,8,2,80,128]{4,3,2,1,0:T(8,128)(2,1)S(1)}, bf16[2,8,2,80,128]{4,3,2,1,0:T(8,128)(2,1)}, u32[]{:S(2)}) copy-start(bf16[2,8,2,80,128]{4,3,2,1,0:T(8,128)(2,1)} %param.24) | copy-start | bytes 1966084
  6.5 103.5 %all-gather.3.cloned.1.call-start = ((), (), s32[]{:S(2)}) async-start(), calls=%async_computation.1 | async-start | bytes 5898240 | tf_op jit(solution)/shard_map/all_gather | solution.py:671
  8.9 9.9 %collective-permute-start = (bf16[80,960]{1,0:T(8,128)(2,1)}, bf16[80,960]{1,0:T(8,128)(2,1)S(1)}, u32[]{:S(2)}, u32[]{:S(2)}) collective-permute-start(bf16[80,960]{1,0:T(8,128)(2,1)} %get-tuple-element.42), channel_id=1, source_target_pairs={{0,1},{1,0},{2,3},{3,2},{4,5},{5,4},{6,7},{7,6},{8,9},{9,8},{10,11... | collective-permute-start | bytes 460808 | tf_op jit(solution)/shard_map/ppermute | solution.py:65
  11.9 15.3 %collective-permute-start.1 = (bf16[80,960]{1,0:T(8,128)(2,1)}, bf16[80,960]{1,0:T(8,128)(2,1)S(1)}, u32[]{:S(2)}, u32[]{:S(2)}) collective-permute-start(bf16[80,960]{1,0:T(8,128)(2,1)} %get-tuple-element.43), channel_id=1, source_target_pairs={{0,2},{1,3},{2,0},{3,1},{4,6},{5,7},{6,4},{7,5},{8,10},{9,11},{10,... | collective-permute-start | bytes 460808 | tf_op jit(solution)/shard_map/ppermute | solution.py:65
  14.5 12.7 %collective-permute-start.2 = (bf16[80,960]{1,0:T(8,128)(2,1)}, bf16[80,960]{1,0:T(8,128)(2,1)S(1)}, u32[]{:S(2)}, u32[]{:S(2)}) collective-permute-start(bf16[80,960]{1,0:T(8,128)(2,1)} %get-tuple-element.44), channel_id=1, source_target_pairs={{0,3},{1,2},{2,1},{3,0},{4,7},{5,6},{6,5},{7,4},{8,11},{9,10},{10,... | collective-permute-start | bytes 460808 | tf_op jit(solution)/shard_map/ppermute | solution.py:65
  27.1 2.6 copy-start.13
  31.4 5.0 %copy-start.22 = (s32[8]{0:T(128)S(1)}, s32[8]{0:T(128)}, u32[]{:S(2)}) copy-start(s32[8]{0:T(128)} %param.26) | copy-start | bytes 100
  31.4 5.7 %copy-start.23 = (s32[8]{0:T(128)S(1)}, s32[8]{0:T(128)}, u32[]{:S(2)}) copy-start(s32[8]{0:T(128)} %param.27) | copy-start | bytes 100
  32.6 28.9 %all-to-all-start = ((bf16[2,16,2,80,128]{4,3,2,0,1:T(8,128)(2,1)}), bf16[2,16,2,80,128]{4,3,2,0,1:T(8,128)(2,1)S(1)}, u32[]{:S(2)}, u32[]{:S(2)}) async-start(bf16[2,16,2,80,128]{4,3,2,0,1:T(8,128)(2,1)} %select_bitcast_fusion), calls=%async_computation | async-start | bytes 2621440 | tf_op jit(solution)/shard_map/all_to_all | solution.py:641
  36.4 239.2 %all-gather.5.cloned.1.call-start = ((), (), s32[]{:S(2)}) async-start(), calls=%async_computation.2 | async-start | bytes 19906560 | tf_op jit(solution)/shard_map/all_gather | solution.py:675
  37.9 8.6 %copy-start.2 = (bf16[512,2560]{1,0:T(8,128)(2,1)S(1)}, bf16[512,2560]{1,0:T(8,128)(2,1)}, u32[]{:S(2)}) copy-start(bf16[512,2560]{1,0:T(8,128)(2,1)} %tokens_ref.1) | copy-start | bytes 7864324
  44.3 4.7 %copy-start.12 = (f32[2560]{0:T(1024)S(1)}, f32[2560]{0:T(1024)}, u32[]{:S(2)}) copy-start(f32[2560]{0:T(1024)} %param.15) | copy-start | bytes 30724
  49.0 15.3 %copy-start.21 = (bf16[80,3456]{1,0:T(8,128)(2,1)S(1)}, bf16[80,3456]{1,0:T(8,128)(2,1)}, u32[]{:S(2)}) copy-start(bf16[80,3456]{1,0:T(8,128)(2,1)} %get-tuple-element.59) | copy-start | bytes 1658884
  49.0 16.3 %copy-start.20 = (bf16[80,3456]{1,0:T(8,128)(2,1)S(1)}, bf16[80,3456]{1,0:T(8,128)(2,1)}, u32[]{:S(2)}) copy-start(bf16[80,3456]{1,0:T(8,128)(2,1)} %get-tuple-element.60) | copy-start | bytes 1658884
  51.1 53.2 %copy-start.9 = (bf16[80,3456]{1,0:T(8,128)(2,1)S(1)}, bf16[80,3456]{1,0:T(8,128)(2,1)}, u32[]{:S(2)}) copy-start(bf16[80,3456]{1,0:T(8,128)(2,1)} %get-tuple-element.57) | copy-start | bytes 1658884
  61.6 22.3 %collective-permute-start.6 = (bf16[80,3456]{1,0:T(8,128)(2,1)}, bf16[80,3456]{1,0:T(8,128)(2,1)S(1)}, u32[]{:S(2)}, u32[]{:S(2)}) collective-permute-start(bf16[80,3456]{1,0:T(8,128)(2,1)} %get-tuple-element.58), channel_id=1, source_target_pairs={{0,1},{1,0},{2,3},{3,2},{4,5},{5,4},{6,7},{7,6},{8,9},{9,8},{10,11... | collective-permute-start | bytes 1658888 | tf_op jit(solution)/shard_map/ppermute | solution.py:65
  64.2 40.1 %collective-permute-start.7 = (bf16[80,3456]{1,0:T(8,128)(2,1)S(1)}, bf16[80,3456]{1,0:T(8,128)(2,1)S(1)}, u32[]{:S(2)}, u32[]{:S(2)}) collective-permute-start(bf16[80,3456]{1,0:T(8,128)(2,1)S(1)} %copy-done.21), channel_id=1, source_target_pairs={{0,2},{1,3},{2,0},{3,1},{4,6},{5,7},{6,4},{7,5},{8,10},{9,11},{10,... | collective-permute-start | bytes 1658888 | tf_op jit(solution)/shard_map/ppermute | solution.py:65
  65.2 39.1 %collective-permute-start.8 = (bf16[80,3456]{1,0:T(8,128)(2,1)S(1)}, bf16[80,3456]{1,0:T(8,128)(2,1)S(1)}, u32[]{:S(2)}, u32[]{:S(2)}) collective-permute-start(bf16[80,3456]{1,0:T(8,128)(2,1)S(1)} %copy-done.20), channel_id=1, source_target_pairs={{0,3},{1,2},{2,1},{3,0},{4,7},{5,6},{6,5},{7,4},{8,11},{9,10},{10,... | collective-permute-start | bytes 1658888 | tf_op jit(solution)/shard_map/ppermute | solution.py:65
  111.1 36.9 %collective-permute-start.10 = (bf16[80,2560]{1,0:T(8,128)(2,1)S(1)}, bf16[80,2560]{1,0:T(8,128)(2,1)S(1)}, u32[]{:S(2)}, u32[]{:S(2)}) collective-permute-start(bf16[80,2560]{1,0:T(8,128)(2,1)S(1)} %constant_dynamic-slice_fusion), channel_id=1, source_target_pairs={{0,2},{1,3},{2,0},{3,1},{4,6},{5,7},{6,4},{7,5},{8,10},{9,11},{10,... | collective-permute-start | bytes 1228808 | tf_op jit(solution)/shard_map/ppermute | solution.py:65
  120.4 27.7 %collective-permute-start.11 = (bf16[80,2560]{1,0:T(8,128)(2,1)S(1)}, bf16[80,2560]{1,0:T(8,128)(2,1)S(1)}, u32[]{:S(2)}, u32[]{:S(2)}) collective-permute-start(bf16[80,2560]{1,0:T(8,128)(2,1)S(1)} %constant_dynamic-slice_fusion), channel_id=1, source_target_pairs={{0,3},{1,2},{2,1},{3,0},{4,7},{5,6},{6,5},{7,4},{8,11},{9,10},{10,... | collective-permute-start | bytes 1228808 | tf_op jit(solution)/shard_map/ppermute | solution.py:65
  121.7 26.4 %collective-permute-start.9 = (bf16[80,2560]{1,0:T(8,128)(2,1)S(1)}, bf16[80,2560]{1,0:T(8,128)(2,1)S(1)}, u32[]{:S(2)}, u32[]{:S(2)}) collective-permute-start(bf16[80,2560]{1,0:T(8,128)(2,1)S(1)} %constant_dynamic-slice_fusion), channel_id=1, source_target_pairs={{0,1},{1,0},{2,3},{3,2},{4,5},{5,4},{6,7},{7,6},{8,9},{9,8},{10,11... | collective-permute-start | bytes 1228808 | tf_op jit(solution)/shard_map/ppermute | solution.py:65
  148.2 17.9 %copy-start.4 = (bf16[3,80,2560]{2,1,0:T(8,128)(2,1)}, bf16[3,80,2560]{2,1,0:T(8,128)(2,1)S(1)}, u32[]{:S(2)}) copy-start(bf16[3,80,2560]{2,1,0:T(8,128)(2,1)S(1)} %pad_maximum_fusion.1.refs_5_) | copy-start | bytes 3686404
  148.2 56.3 %collective-permute-start.12 = (bf16[3,80,2560]{2,1,0:T(8,128)(2,1)S(1)}, bf16[3,80,2560]{2,1,0:T(8,128)(2,1)S(1)}, u32[]{:S(2)}, u32[]{:S(2)}) collective-permute-start(bf16[3,80,2560]{2,1,0:T(8,128)(2,1)S(1)} %pad_maximum_fusion.1.refs_5_), channel_id=1, source_target_pairs={{0,8},{4,12},{8,0},{12,4},{16,24},{20,28},{24,16},{28,20},{1,9},{5... | collective-permute-start | bytes 3686408 | tf_op jit(solution)/shard_map/ppermute | solution.py:65
  152.3 52.3 %collective-permute-start.13 = (bf16[3,80,2560]{2,1,0:T(8,128)(2,1)S(1)}, bf16[3,80,2560]{2,1,0:T(8,128)(2,1)S(1)}, u32[]{:S(2)}, u32[]{:S(2)}) collective-permute-start(bf16[3,80,2560]{2,1,0:T(8,128)(2,1)S(1)} %pad_maximum_fusion.1.refs_5_), channel_id=1, source_target_pairs={{0,16},{4,20},{8,24},{12,28},{16,0},{20,4},{24,8},{28,12},{1,17},{... | collective-permute-start | bytes 3686408 | tf_op jit(solution)/shard_map/ppermute | solution.py:65
  152.3 13.8 %copy-start.10 = (bf16[256,640]{1,0:T(8,128)(2,1)S(1)}, bf16[256,640]{1,0:T(8,128)(2,1)}, u32[]{:S(2)}) copy-start(bf16[256,640]{1,0:T(8,128)(2,1)} %attention.2) | copy-start | bytes 983044
  167.2 37.4 %copy-start.7 = (bf16[512,640]{1,0:T(8,128)(2,1)}, bf16[512,640]{1,0:T(8,128)(2,1)S(1)}, u32[]{:S(2)}) copy-start(bf16[512,640]{1,0:T(8,128)(2,1)S(1)} %pad_maximum_fusion.3.refs_0_) | copy-start | bytes 1966084
  167.2 33.2 %collective-permute-start.3 = (bf16[512,640]{1,0:T(8,128)(2,1)S(1)}, bf16[512,640]{1,0:T(8,128)(2,1)S(1)}, u32[]{:S(2)}, u32[]{:S(2)}) collective-permute-start(bf16[512,640]{1,0:T(8,128)(2,1)S(1)} %pad_maximum_fusion.3.refs_0_), channel_id=1, source_target_pairs={{0,1},{1,0},{2,3},{3,2},{4,5},{5,4},{6,7},{7,6},{8,9},{9,8},{10,11... | collective-permute-start | bytes 1966088 | tf_op jit(solution)/shard_map/ppermute | solution.py:65
  174.6 29.9 %collective-permute-start.4 = (bf16[512,640]{1,0:T(8,128)(2,1)S(1)}, bf16[512,640]{1,0:T(8,128)(2,1)S(1)}, u32[]{:S(2)}, u32[]{:S(2)}) collective-permute-start(bf16[512,640]{1,0:T(8,128)(2,1)S(1)} %pad_maximum_fusion.3.refs_0_), channel_id=1, source_target_pairs={{0,2},{1,3},{2,0},{3,1},{4,6},{5,7},{6,4},{7,5},{8,10},{9,11},{10,... | collective-permute-start | bytes 1966088 | tf_op jit(solution)/shard_map/ppermute | solution.py:65
  174.7 79.1 %copy-start.11 = (f32[2560]{0:T(1024)S(1)}, f32[2560]{0:T(1024)}, u32[]{:S(2)}) copy-start(f32[2560]{0:T(1024)} %param.16) | copy-start | bytes 30724
  200.4 4.4 %copy-start.17 = (bf16[512,640]{1,0:T(8,128)(2,1)}, bf16[512,640]{1,0:T(8,128)(2,1)S(1)}, u32[]{:S(2)}) copy-start(bf16[512,640]{1,0:T(8,128)(2,1)S(1)} %collective-permute-done.3.refs_1_) | copy-start | bytes 1966084
  204.5 2.1 copy-start.18
  204.5 1.1 copy-start.5
  204.5 1.5 copy-start.6
  205.6 51.1 %collective-permute-start.15 = (bf16[9,80,2560]{2,1,0:T(8,128)(2,1)S(1)}, bf16[9,80,2560]{2,1,0:T(8,128)(2,1)S(1)}, u32[]{:S(2)}, u32[]{:S(2)}) collective-permute-start(bf16[9,80,2560]{2,1,0:T(8,128)(2,1)S(1)} %constant_dynamic-update-slice_fusion), channel_id=1, source_target_pairs={{0,4},{4,0},{8,12},{12,8},{16,20},{20,16},{24,28},{28,24},{1,5},{5... | collective-permute-start | bytes 11059208 | tf_op jit(solution)/shard_map/ppermute | solution.py:65
  206.0 47.7 %collective-permute-start.14 = (bf16[3,80,2560]{2,1,0:T(8,128)(2,1)S(1)}, bf16[3,80,2560]{2,1,0:T(8,128)(2,1)S(1)}, u32[]{:S(2)}, u32[]{:S(2)}) collective-permute-start(bf16[3,80,2560]{2,1,0:T(8,128)(2,1)S(1)} %collective-permute-done.13.refs_7_), channel_id=1, source_target_pairs={{0,8},{4,12},{8,0},{12,4},{16,24},{20,28},{24,16},{28,20},{1,9},{5... | collective-permute-start | bytes 3686408 | tf_op jit(solution)/shard_map/ppermute | solution.py:65
  206.6 18.3 %collective-permute-start.5 = (bf16[512,640]{1,0:T(8,128)(2,1)S(1)}, bf16[512,640]{1,0:T(8,128)(2,1)S(1)}, u32[]{:S(2)}, u32[]{:S(2)}) collective-permute-start(bf16[512,640]{1,0:T(8,128)(2,1)S(1)} %collective-permute-done.4.refs_2_), channel_id=1, source_target_pairs={{0,1},{1,0},{2,3},{3,2},{4,5},{5,4},{6,7},{7,6},{8,9},{9,8},{10,11... | collective-permute-start | bytes 1966088 | tf_op jit(solution)/shard_map/ppermute | solution.py:65
  225.0 31.7 %copy-start.19 = (bf16[512,640]{1,0:T(8,128)(2,1)}, bf16[512,640]{1,0:T(8,128)(2,1)S(1)}, u32[]{:S(2)}) copy-start(bf16[512,640]{1,0:T(8,128)(2,1)S(1)} %collective-permute-done.5.refs_3_) | copy-start | bytes 1966084
  253.8 2.9 copy-start.15
  253.8 2.9 collective-permute-start.16
  256.7 1.1 copy-start.16
  257.7 1.9 copy-start.14
  296.7 54.8 %copy-start.3 = (f32[512,640]{1,0:T(8,128)S(1)}, f32[512,640]{1,0:T(8,128)}, u32[]{:S(2)}) copy-start(f32[512,640]{1,0:T(8,128)} %get-tuple-element.71) | copy-start | bytes 3932164
  296.7 54.8 %copy-start.8 = (bf16[512,640]{1,0:T(8,128)(2,1)S(1)}, bf16[512,640]{1,0:T(8,128)(2,1)}, u32[]{:S(2)}) copy-start(bf16[512,640]{1,0:T(8,128)(2,1)} %get-tuple-element.68) | copy-start | bytes 1966084
  296.7 21.0 %collective-permute-start.17 = (bf16[512,640]{1,0:T(8,128)(2,1)}, bf16[512,640]{1,0:T(8,128)(2,1)S(1)}, u32[]{:S(2)}, u32[]{:S(2)}) collective-permute-start(bf16[512,640]{1,0:T(8,128)(2,1)} %get-tuple-element.73), channel_id=1, source_target_pairs={{0,1},{1,0},{2,3},{3,2},{4,5},{5,4},{6,7},{7,6},{8,9},{9,8},{10,11... | collective-permute-start | bytes 1966088 | tf_op jit(solution)/shard_map/ppermute | solution.py:65
  317.7 27.6 %collective-permute-start.18 = (bf16[512,640]{1,0:T(8,128)(2,1)}, bf16[512,640]{1,0:T(8,128)(2,1)S(1)}, u32[]{:S(2)}, u32[]{:S(2)}) collective-permute-start(bf16[512,640]{1,0:T(8,128)(2,1)} %get-tuple-element.74), channel_id=1, source_target_pairs={{0,1},{1,0},{2,3},{3,2},{4,5},{5,4},{6,7},{7,6},{8,9},{9,8},{10,11... | collective-permute-start | bytes 1966088 | tf_op jit(solution)/shard_map/ppermute | solution.py:65
  319.4 33.2 %copy-start.1 = (bf16[2,8,2,80,128]{4,3,2,1,0:T(8,128)(2,1)S(1)}, bf16[2,8,2,80,128]{4,3,2,1,0:T(8,128)(2,1)}, u32[]{:S(2)}) copy-start(bf16[2,8,2,80,128]{4,3,2,1,0:T(8,128)(2,1)} %param.24) | copy-start | bytes 1966084
  320.8 30.7 %collective-permute-start.19 = (bf16[512,640]{1,0:T(8,128)(2,1)S(1)}, bf16[512,640]{1,0:T(8,128)(2,1)S(1)}, u32[]{:S(2)}, u32[]{:S(2)}) collective-permute-start(bf16[512,640]{1,0:T(8,128)(2,1)S(1)} %add_convert_fusion), channel_id=1, source_target_pairs={{0,2},{1,3},{2,0},{3,1},{4,6},{5,7},{6,4},{7,5},{8,10},{9,11},{10,... | collective-permute-start | bytes 1966088 | tf_op jit(solution)/shard_map/ppermute | solution.py:65
Sparse Core Ops, SparseCore 0:
  29.9 54.5 all-gather.2
  110.2 137.4 all-gather.4
